TPU v7x, 128 devices: a whole 4x4x4 slice. The times are simulated.
128 devices in a mesh: fsdp: 16 (over z_hi, x, core), tp: 8 (over z_lo, y).
Axes of the slice: x: 4, y: 4, z: 4 (z_hi: 2, z_lo: 2; z = z_hi * 2 + z_lo), core: 2. Of those that a mesh axis runs over, the one named last changes fastest.
Arguments:
- master: float32 [4096, 15360], P(('fsdp', 'tp')), may hold values from -0.09375 to 0.09375
- queries: bfloat16 [128, 8, 4096], P('fsdp', None, 'tp'), may hold values from -100 to 100
- new_token_key_value: bfloat16 [128, 8, 2, 1024], P('fsdp', None, None, 'tp'), may hold values from -6 to 6
- out_weight: bfloat16 [4096, 4096], P('tp'), may hold values from -0.09375 to 0.09375
- kv_cache: bfloat16 [128, 2, 8, 1024, 128], P('fsdp', None, 'tp'), may hold values from -8 to 8
- lengths: int32 [128], P('fsdp'), may hold values from 2 to 1024
Outputs:
- new_weight: bfloat16 [4096, 15360], P(None, 'tp')
- attn_out: bfloat16 [128, 8, 4096], P('fsdp', None, 'tp')
All inputs are finite; a program needn't handle non-finite values.
Results may differ from a plain program's by a relative error of at most 0.0057.
Values may be sent and summed in bfloat16 or wider, within the bound.
No kernel may reach another device: no remote copies, remote signals or barrier semaphores. Data moves between devices by JAX's collectives and lax.ppermute only.
A program may use at most 128 MiB of HBM per device.

v0:
```python
import math

import jax
import jax.numpy as jnp
from jax import lax
from jax.sharding import PartitionSpec as P


def attend_local(queries, new_token_key_value, kv_cache, lengths):
    rows, steps, width = queries.shape
    head_dim = kv_cache.shape[-1]
    kv_heads = kv_cache.shape[2]
    span = kv_cache.shape[3]
    group = width // head_dim // kv_heads
    fresh = new_token_key_value.reshape(rows, steps, 2, kv_heads, head_dim)
    query_heads = queries.reshape(rows, steps, kv_heads, group, head_dim)
    scale = 1.0 / math.sqrt(head_dim)
    old_scores = (
        jnp.einsum(
            "rsgqe,rgle->rsgql", query_heads, kv_cache[:, 0], preferred_element_type=jnp.float32
        )
        * scale
    )
    new_scores = (
        jnp.einsum(
            "rsgqe,rnge->rsgqn", query_heads, fresh[:, :, 0], preferred_element_type=jnp.float32
        )
        * scale
    )
    old_valid = (jnp.arange(span)[None, :] < lengths[:, None])[:, None, None, None, :]
    new_valid = (jnp.arange(steps)[None, :] <= jnp.arange(steps)[:, None])[None, :, None, None, :]
    old_scores = jnp.where(old_valid, old_scores, jnp.float32(-1e30))
    new_scores = jnp.where(new_valid, new_scores, jnp.float32(-1e30))
    top = jnp.maximum(
        jnp.max(old_scores, axis=-1, keepdims=True), jnp.max(new_scores, axis=-1, keepdims=True)
    )
    old_exp = jnp.exp(old_scores - top)
    new_exp = jnp.exp(new_scores - top)
    total = jnp.sum(old_exp, axis=-1, keepdims=True) + jnp.sum(new_exp, axis=-1, keepdims=True)
    old_weights = (old_exp / total).astype(jnp.bfloat16)
    new_weights = (new_exp / total).astype(jnp.bfloat16)
    mixed = jnp.einsum(
        "rsgql,rgle->rsgqe", old_weights, kv_cache[:, 1], preferred_element_type=jnp.float32
    )
    mixed = mixed + jnp.einsum(
        "rsgqn,rnge->rsgqe", new_weights, fresh[:, :, 1], preferred_element_type=jnp.float32
    )
    return mixed.astype(jnp.bfloat16).reshape(rows, steps, width)


def local(master, queries, new_token_key_value, out_weight, kv_cache, lengths):
    narrow = master.astype(jnp.bfloat16)
    local_rows = lax.all_to_all(narrow, "tp", split_axis=1, concat_axis=0, tiled=True)
    new_weight = lax.all_gather(local_rows, "fsdp", axis=0, tiled=True)
    attn_heads = attend_local(queries, new_token_key_value, kv_cache, lengths)
    partial_out = jnp.einsum(
        "rsw,wd->rsd", attn_heads, out_weight, preferred_element_type=jnp.float32
    )
    attn_out = lax.psum_scatter(partial_out, "tp", scatter_dimension=2, tiled=True).astype(
        jnp.bfloat16
    )
    return (new_weight, attn_out)


def solution(mesh):
    in_specs = (
        P(("fsdp", "tp"), None),
        P("fsdp", None, "tp"),
        P("fsdp", None, None, "tp"),
        P("tp", None),
        P("fsdp", None, "tp", None, None),
        P("fsdp"),
    )
    out_specs = (P(None, "tp"), P("fsdp", None, "tp"))
    return jax.shard_map(local, mesh=mesh, in_specs=in_specs, out_specs=out_specs, check_vma=False)
```

profile of v0, /device:TPU:1, one launch (start us, length us, event | category | flops | bytes accessed | tf_op | source)
XLA Modules:
  0.0 170.8 jit_solution(478828001020238989)
XLA Ops:
  8.0 0.0 copy-start
  8.0 0.0 reduce-scatter.2.cloned.1.call-start
  8.1 0.8 copy.24
  8.8 0.7 iota_compare_fusion
  9.6 0.0 copy-done
  9.6 0.4 fusion.45
  10.0 2.5 %fusion.44 = (f32[8,8,4]{1,2,0:T(4,128)S(1)}, f32[8,8,1,4,1024]{4,1,3,0,2:T(8,128)S(1)}) fusion(bf16[8,8,512]{2,1,0:T(8,128)(2,1)S(1)} %copy-done, bf16[8,2,1,1024,128]{4,3,2,1,0:T(8,128)(2,1)} %param.10, pred[8,1024]{1,0:T(8,128)(4,1)S(1)} %iota_compare_fusion), kind=kOutput, calls=%fused_computation.37 | convolution fusion | flops 67895040 | bytes 3220480 | tf_op jit(solution)/shard_map/rsgqe,rgle->rsgql/dot_general | solution.py:19
  12.5 0.3 fusion.31
  12.8 0.1 fusion.38
  12.9 0.2 fusion.39
  13.1 0.0 copy-start.1
  13.1 5.2 %fusion = f32[8,8,4096]{2,1,0:T(8,128)} fusion(bf16[512,4096]{1,0:T(8,128)(2,1)} %param.9, f32[8,8,4,128]{3,1,2,0:T(8,128)S(1)} %fusion.39, bf16[8,2,1,1024,128]{4,3,2,1,0:T(8,128)(2,1)} %param.10, f32[8,8,1,4,1024]{4,1,3,0,2:T(8,128)S(1)} %get-tuple-element.3, f32[8,8,4]{1,2,0:T(4,128)S(1)} %add.16, f32[8,8,4]{1,2,0:T(4,128)S(1)} %max.8), kind=kOutput, calls=%fused_computation | convolution fusion | flops 336396288 | bytes 8521728 | tf_op jit(solution)/shard_map/rsw,wd->rsd/dot_general | solution.py:56
  18.3 0.0 reduce-scatter.2.cloned.1.call-update
  18.3 0.0 all-gather.2.cloned.1.call-start
  18.4 0.0 copy-done.1
  18.4 0.1 convert_element_type.24
  18.5 0.1 copy.23
  18.6 22.3 %all_to_all.19 = bf16[32,8,1920]{2,0,1:T(8,128)(2,1)} all-to-all(bf16[32,8,1920]{2,0,1:T(8,128)(2,1)S(1)} %bitcast.106), channel_id=1, replica_groups=mesh['fsdp'=16,'tp'=8] {'tp'}, dimensions={1} | all-to-all | bytes 1966080 | tf_op jit(solution)/shard_map/all_to_all | solution.py:53
  40.9 0.0 all-gather.2.cloned.1.call-update
  41.0 18.7 %reduce-scatter.2.cloned.1.call-done = f32[8,8,512]{2,1,0:T(8,128)} async-done(((f32[8,8,4096]{2,1,0:T(8,128)}), f32[8,8,512]{2,1,0:T(8,128)}) %reduce-scatter.2.cloned.1.call-update) | async-done | bytes 131088 | tf_op jit(solution)/shard_map/reduce_scatter | solution.py:59
  59.7 1.5 convert_element_type.31
  61.2 88.9 %all-gather.2.cloned.1.call-done = bf16[4096,1920]{1,0:T(8,128)(2,1)} async-done(((bf16[256,1920]{1,0:T(8,128)(2,1)}), bf16[4096,1920]{1,0:T(8,128)(2,1)}) %all-gather.2.cloned.1.call-update) | async-done | bytes 15728656 | tf_op jit(solution)/shard_map/all_gather | solution.py:54
  150.1 13.2 %copy.26 = bf16[4096,1920]{1,0:T(8,128)(2,1)} copy(bf16[4096,1920]{1,0:T(8,128)(2,1)} %all-gather.2.cloned.1.call-done) | data formatting | bytes 31457280
  (3 shorter events, 0.0 us)
Async XLA Ops:
  8.0 1.6 copy-start
  8.0 51.7 %reduce-scatter.2.cloned.1.call-start = ((), (), s32[]{:S(2)}) async-start(), calls=%async_computation.3 | async-start | bytes 1179648 | tf_op jit(solution)/shard_map/reduce_scatter | solution.py:59
  13.1 5.3 %copy-start.1 = (f32[32,15360]{1,0:T(8,128)S(1)}, f32[32,15360]{1,0:T(8,128)}, u32[]{:S(2)}) copy-start(f32[32,15360]{1,0:T(8,128)} %param.6) | copy-start | bytes 5898244
  18.3 131.8 %all-gather.2.cloned.1.call-start = ((), (), s32[]{:S(2)}) async-start(), calls=%async_computation.2 | async-start | bytes 16711680 | tf_op jit(solution)/shard_map/all_gather | solution.py:54
Sparse Core Ops, SparseCore 0:
  18.5 41.1 reduce-scatter.1
Sparse Core Ops, SparseCore 1:
  41.0 109.0 all-gather.1
where the time goes:
time: 171 us
  waiting for transfers between devices  108 us (63%)
  blocking collectives  22.3 us (13%)
  between operations  15.5 us (9%)
  local copies, waits for them, and re-layouts  14.1 us (8%)
  matrix products  8.33 us (5%)
  other arithmetic  2.78 us (2%)
    all_gather x1, waiting for transfers between devices, local(): new_weight = lax.all_gather(local_rows, 'fsdp', axis=0, tiled=True)  88.9 us
    all_to_all x1, blocking collectives, local(): lax.all_to_all(narrow, 'tp', split_axis=1, concat_axis=0, tiled=True)  22.3 us
    reduce_scatter x1, waiting for transfers between devices, local(): lax.psum_scatter(partial_out, 'tp', scatter_dimension=2, tiled=True)  18.7 us
    unnamed x6, local copies, waits for them, and re-layouts  14 us
    dot_general x1, matrix products, local(): jnp.einsum('rsw,wd->rsd', attn_heads, out_weight, preferred_element_type=...  5.21 us
  transfers between devices with their start and end apart: 2, of which 2 were waited for; matrix products, arithmetic and copies ran while one was open for 1% of the time, Pallas kernels for 0%

commit v1 on v0

v1 whole, which is shorter than its diff:
```python
import math

import jax
import jax.numpy as jnp
from jax import lax
from jax.experimental import pallas as pl
from jax.experimental.pallas import tpu as pltpu
from jax.sharding import PartitionSpec as P

AXES = ("fsdp", "tp")

def send(value, dx=0, dy=0, dz=0, dc=0):
    pairs = []
    for z in range(4):
        for x in range(4):
            for c in range(2):
                for y in range(4):
                    z2, x2, c2, y2 = (z + dz) % 4, (x + dx) % 4, (c + dc) % 2, (y + dy) % 4
                    source = ((z // 2 * 4 + x) * 2 + c) * 8 + z % 2 * 4 + y
                    target = ((z2 // 2 * 4 + x2) * 2 + c2) * 8 + z2 % 2 * 4 + y2
                    pairs.append((source, target))
    return lax.ppermute(value, AXES, pairs)


def cast_blocks(master):
    rows, width = master.shape[0], master.shape[1] // 8

    def kernel(in_ref, out_ref):
        for t in range(8):
            out_ref[t] = in_ref[:, t * width : (t + 1) * width].astype(jnp.bfloat16)

    whole = pl.BlockSpec(memory_space=pltpu.VMEM)
    return pl.pallas_call(
        kernel,
        in_specs=[whole],
        out_specs=whole,
        out_shape=jax.ShapeDtypeStruct((8, rows, width), jnp.bfloat16),
        compiler_params=pltpu.CompilerParams(vmem_limit_bytes=16 << 20),
    )(master)


def attend(queries, fresh, kv_cache, out_weight, lengths, after):
    rows, steps, width = queries.shape
    span, head = kv_cache.shape[3:]
    group = width // head
    part = out_weight.shape[1] // 8
    scale = 1.0 / math.sqrt(head)

    def kernel(lengths_ref, q_ref, fresh_ref, cache_hbm, weight_hbm, after_ref, out_ref, *scratch):
        cache_ref, weight_ref, heads_ref, cache_sem, weight_sem = scratch
        caches = [
            pltpu.make_async_copy(cache_hbm.at[r, :, 0], cache_ref.at[r], cache_sem.at[r])
            for r in range(rows)
        ]
        weights = [
            pltpu.make_async_copy(
                weight_hbm.at[:, pl.ds(t * part, part)], weight_ref.at[t], weight_sem.at[t]
            )
            for t in range(8)
        ]
        for copy in caches + weights:
            copy.start()
        contract = (((1,), (1,)), ((), ()))
        for r in range(rows):
            q = q_ref[r].astype(jnp.float32)
            q = jnp.concatenate([q[:, h * head : (h + 1) * head] for h in range(group)], 0)
            q = q.astype(jnp.bfloat16)
            caches[r].wait()
            old = lax.dot_general(q, cache_ref[r, 0], contract, preferred_element_type=jnp.float32)
            new = lax.dot_general(
                q, fresh_ref[r, :, 0], contract, preferred_element_type=jnp.float32
            )
            place = lax.broadcasted_iota(jnp.int32, old.shape, 1)
            old = jnp.where(place < lengths_ref[r], old * scale, jnp.float32(-1e30))
            step = lax.rem(lax.broadcasted_iota(jnp.int32, new.shape, 0), steps)
            token = lax.broadcasted_iota(jnp.int32, new.shape, 1)
            new = jnp.where(token <= step, new * scale, jnp.float32(-1e30))
            top = jnp.maximum(
                jnp.max(old, axis=1, keepdims=True), jnp.max(new, axis=1, keepdims=True)
            )
            old, new = jnp.exp(old - top), jnp.exp(new - top)
            total = jnp.sum(old, axis=1, keepdims=True) + jnp.sum(new, axis=1, keepdims=True)
            old = (old / total).astype(jnp.bfloat16)
            new = (new / total).astype(jnp.bfloat16)
            mixed = jnp.dot(old, cache_ref[r, 1], preferred_element_type=jnp.float32)
            mixed += jnp.dot(new, fresh_ref[r, :, 1], preferred_element_type=jnp.float32)
            for h in range(group):
                heads_ref[r * steps : (r + 1) * steps, h * head : (h + 1) * head] = mixed[
                    h * steps : (h + 1) * steps
                ]
        heads = heads_ref[...].astype(jnp.bfloat16)
        for t in range(8):
            weights[t].wait()
            out_ref[t % 4, t // 4] = jnp.dot(
                heads, weight_ref[t], preferred_element_type=jnp.float32
            )

    vmem, hbm = pl.BlockSpec(memory_space=pltpu.VMEM), pl.BlockSpec(memory_space=pltpu.HBM)
    return pl.pallas_call(
        kernel,
        in_specs=[
            pl.BlockSpec(memory_space=pltpu.SMEM), vmem, vmem, hbm, hbm,
            pl.BlockSpec(memory_space=pl.ANY),
        ],
        out_specs=vmem,
        out_shape=jax.ShapeDtypeStruct((4, 2, rows * steps, part), jnp.float32),
        scratch_shapes=[
            pltpu.VMEM((rows, 2, span, head), jnp.bfloat16),
            pltpu.VMEM((8, width, part), jnp.bfloat16),
            pltpu.VMEM((rows * steps, width), jnp.float32),
            pltpu.SemaphoreType.DMA((rows,)),
            pltpu.SemaphoreType.DMA((8,)),
        ],
        compiler_params=pltpu.CompilerParams(vmem_limit_bytes=16 << 20),
        cost_estimate=pl.CostEstimate(flops=1, bytes_accessed=1, transcendentals=0),
    )(
        lengths,
        queries,
        fresh,
        pltpu.with_memory_space_constraint(kv_cache, pltpu.HBM),
        pltpu.with_memory_space_constraint(out_weight, pltpu.HBM),
        after,
    )


def place(out, pieces):
    shape = (2, 4, 2, 8) + pieces[0][0].shape[1:]
    index = jnp.stack([jnp.int32(v) for p in pieces for v in p[2:]])
    count = len(pieces)

    def kernel(index_ref, *refs):
        out_ref, sem = refs[-2], refs[-1]
        copies = []
        for k in range(count):
            z, x, c = (index_ref[3 * k + j] for j in range(3))
            target = out_ref.at[z, x, c, pl.ds(pieces[k][1], pieces[k][0].shape[0])]
            copies.append(pltpu.make_async_copy(refs[k], target, sem.at[k]))
        for copy in copies:
            copy.start()
        for copy in copies:
            copy.wait()

    operands = [index] + [p[0] for p in pieces] + ([] if out is None else [out])
    specs = [pl.BlockSpec(memory_space=pltpu.SMEM)]
    specs += [pl.BlockSpec(memory_space=pltpu.VMEM)] * count
    specs += [] if out is None else [pl.BlockSpec(memory_space=pl.ANY)]
    return pl.pallas_call(
        kernel,
        in_specs=specs,
        out_specs=pl.BlockSpec(memory_space=pl.ANY),
        out_shape=jax.ShapeDtypeStruct(shape, jnp.bfloat16),
        scratch_shapes=[pltpu.SemaphoreType.DMA((count,))],
        input_output_aliases={} if out is None else {count + 1: 0},
        compiler_params=pltpu.CompilerParams(vmem_limit_bytes=12 << 20),
    )(*operands)


def fence(*values):
    def kernel(*refs):
        pass

    made = pl.pallas_call(
        kernel,
        in_specs=[pl.BlockSpec(memory_space=pl.ANY)] * len(values),
        out_specs=[pl.BlockSpec(memory_space=pl.ANY)] * len(values),
        out_shape=[jax.ShapeDtypeStruct(v.shape, v.dtype) for v in values],
        input_output_aliases={k: k for k in range(len(values))},
        compiler_params=pltpu.CompilerParams(vmem_limit_bytes=1 << 20),
    )(*values)
    return made if len(values) > 1 else made[0]


def local(master, queries, new_token_key_value, out_weight, kv_cache, lengths):
    f, t = lax.axis_index("fsdp"), lax.axis_index("tp")
    z_hi, x, core = f // 8, f // 2 % 4, f % 2
    z_lo = t // 4
    width = master.shape[1] // 8
    blocks = cast_blocks(master)

    def swap(piece):
        with jax.named_scope("core"):
            return send(piece, dc=1)

    def both(piece, z, hop, first=0):
        place_x = (x - hop) % 4
        return [(piece, first, z, place_x, core), (swap(piece), first, z, place_x, 1 - core)]

    def pick(value, index):
        return lax.dynamic_index_in_dim(value, index, 0, keepdims=False)

    with jax.named_scope("over_t"):
        own = lax.all_to_all(blocks, "tp", split_axis=0, concat_axis=0, tiled=True)
    r, s, w = queries.shape
    shares = attend(queries, new_token_key_value, kv_cache, out_weight, lengths, blocks)
    own, shares = fence(own, shares)

    with jax.named_scope("own_x"):
        own_1, own_3 = send(own, dx=1), send(own, dx=-1)
    with jax.named_scope("over_z"):
        dup = send(own, dz=2)
    with jax.named_scope("sum_y"):
        shares = lax.all_to_all(
            shares, "tp", split_axis=0, concat_axis=0, tiled=True,
            axis_index_groups=((0, 1, 2, 3), (4, 5, 6, 7)),
        )
    out = place(None, both(own, z_hi, 0))
    own_1, own_3, shares, out = fence(own_1, own_3, shares, out)

    with jax.named_scope("own_x2"):
        own_2, own_2b = send(own_1[:4], dx=1), send(own_3[4:], dx=-1)
    with jax.named_scope("dup_x"):
        dup_1, dup_3 = send(dup, dx=1), send(dup, dx=-1)
    with jax.named_scope("sum_z"):
        total = jnp.sum(shares, axis=0)
        pairs = [(i, i // 8 * 8 + (i + 4) % 8) for i in range(128)]
        attn = pick(total, z_lo) + lax.ppermute(pick(total, 1 - z_lo), AXES, pairs)
        attn = attn.astype(jnp.bfloat16)
    out = place(out, both(own_1, z_hi, 1) + both(own_3, z_hi, 3))
    own_2, own_2b, attn, out = fence(own_2, own_2b, attn, out)

    with jax.named_scope("over_z2"):
        dup_2, dup_2b = send(own_2, dz=2), send(own_2b, dz=2)
    out = place(out, both(dup, 1 - z_hi, 0) + both(own_2, z_hi, 2) + both(own_2b, z_hi, 2, 4))
    dup_1, dup_2, dup_2b, dup_3, out = fence(dup_1, dup_2, dup_2b, dup_3, out)

    pairs = [both(dup_1, 1 - z_hi, 1), both(dup_3, 1 - z_hi, 3)]
    pairs += [both(dup_2, 1 - z_hi, 2), both(dup_2b, 1 - z_hi, 2, 4)]
    out = place(out, [mine for mine, _ in pairs])
    out = place(out, [theirs for _, theirs in pairs])
    return (out.reshape(-1, width), attn.reshape(r, s, -1))


def solution(mesh):
    in_specs = (
        P(("fsdp", "tp"), None),
        P("fsdp", None, "tp"),
        P("fsdp", None, None, "tp"),
        P("tp", None),
        P("fsdp", None, "tp", None, None),
        P("fsdp"),
    )
    out_specs = (P(None, "tp"), P("fsdp", None, "tp"))
    return jax.shard_map(local, mesh=mesh, in_specs=in_specs, out_specs=out_specs, check_vma=False)
```

time: 171 us -> 108 us (0.63)
  waiting for transfers between devices: 108 us -> 35.5 us
  starting transfers between devices: 0.08 us -> 36.5 us
  Pallas kernels: 0 us -> 25.2 us
  blocking collectives: 22.3 us -> 0 us
  between operations: 15.5 us -> 0.76 us
  matrix products: 8.33 us -> 0 us
  local copies, waits for them, and re-layouts: 14.1 us -> 8.73 us
  other arithmetic: 2.78 us -> 0.74 us
    all_gather x1 -> x0, waiting for transfers between devices: 88.9 us -> none  [local(): new_weight = lax.all_gather(local_rows, 'fsdp', axis=0, tiled=True)]
    ppermute x0 -> x20, starting transfers between devices: none -> 26.7 us  [the longest x19 26.3 us: send(): return lax.ppermute(value, AXES, pairs)]
    pallas_call x0 -> x11, Pallas kernels: none -> 25.2 us  [the longest x5 15.4 us: place(): pl.pallas_call(kernel, in_specs=specs, out_specs=pl.BlockSpec(memory_spac...]
    ppermute x0 -> x20, waiting for transfers between devices: none -> 22.7 us  [the longest x19 21.9 us: send(): return lax.ppermute(value, AXES, pairs)]
    all_to_all x1 -> x0, blocking collectives: 22.3 us -> none  [local(): lax.all_to_all(narrow, 'tp', split_axis=1, concat_axis=0, tiled=True)]
    reduce_scatter x1 -> x0, waiting for transfers between devices: 18.7 us -> none  [local(): lax.psum_scatter(partial_out, 'tp', scatter_dimension=2, tiled=True)]
    all_to_all x0 -> x2, waiting for transfers between devices: none -> 12.8 us  [the longest x1 8.72 us: local(): lax.all_to_all(shares, 'tp', split_axis=0, concat_axis=0, tiled=True, axi...]
    all_to_all x0 -> x2, starting transfers between devices: none -> 9.89 us  [the longest x1 6.37 us: local(): own = lax.all_to_all(blocks, 'tp', split_axis=0, concat_axis=0, tiled=True)]
  transfers between devices with their start and end apart: 2 -> 22, of which waited for: 2 -> 12; matrix products, arithmetic and copies ran while one was open for 1% -> 4% of each run, Pallas kernels for 0% -> 19%
where the time goes in v1:
time: 108 us
  starting transfers between devices  36.5 us (34%)
  waiting for transfers between devices  35.5 us (33%)
  Pallas kernels  25.2 us (23%)
  local copies, waits for them, and re-layouts  8.73 us (8%)
    ppermute x19, starting transfers between devices, send(): return lax.ppermute(value, AXES, pairs)  26.3 us
    ppermute x19, waiting for transfers between devices, send(): return lax.ppermute(value, AXES, pairs)  21.9 us
    pallas_call x5, Pallas kernels, place(): pl.pallas_call(kernel, in_specs=specs, out_specs=pl.BlockSpec(memory_spac...  15.4 us
    pallas_call x1, Pallas kernels, attend(): pl.pallas_call(kernel, in_specs=[pl.BlockSpec(memory_space=pltpu.SMEM), v...  8.77 us
    all_to_all x1, waiting for transfers between devices, local(): lax.all_to_all(shares, 'tp', split_axis=0, concat_axis=0, tiled=True, axi...  8.72 us
    all_to_all x1, starting transfers between devices, local(): own = lax.all_to_all(blocks, 'tp', split_axis=0, concat_axis=0, tiled=True)  6.37 us
    unnamed x12, local copies, waits for them, and re-layouts  5.58 us
    all_to_all x1, waiting for transfers between devices, local(): own = lax.all_to_all(blocks, 'tp', split_axis=0, concat_axis=0, tiled=True)  4.07 us
  transfers between devices with their start and end apart: 22, of which 12 were waited for; matrix products, arithmetic and copies ran while one was open for 4% of the time, Pallas kernels for 19%

profile of v1, /device:TPU:1, one launch (start us, length us, event | category | flops | bytes accessed | tf_op | source)
XLA Modules:
  0.0 107.5 jit_solution(3486120697703206132)
XLA Ops:
  0.6 1.5 %copy-done = f32[32,15360]{1,0:T(8,128)S(1)} copy-done((f32[32,15360]{1,0:T(8,128)S(1)}, f32[32,15360]{1,0:T(8,128)}, u32[]{:S(2)}) %copy-start) | copy-done | bytes 1966104
  2.2 1.0 shard_map.77.after_ref
  3.2 6.4 %all-to-all-start = ((bf16[8,32,1920]{2,1,0:T(8,128)(2,1)}), bf16[8,32,1920]{2,1,0:T(8,128)(2,1)S(1)}, u32[]{:S(2)}, u32[]{:S(2)}) async-start(bf16[8,32,1920]{2,1,0:T(8,128)(2,1)} %shard_map.77.after_ref), calls=%async_computation | async-start | bytes 1966080 | tf_op jit(solution)/shard_map/over_t/all_to_all | solution.py:192
  9.6 0.8 copy-done.3
  11.8 8.8 %shard_map.78.refs_1_ = f32[4,2,64,512]{3,2,1,0:T(8,128)} custom-call(s32[8]{0:T(128)S(1)} %copy-done.5, bf16[8,8,512]{2,1,0:T(8,128)(2,1)S(1)} %copy-done.3, bf16[8,8,2,128]{3,2,1,0:T(2,128)(2,1)S(1)} %copy-done.4, bf16[8,2,1,1024,128]{4,3,2,1,0:T(8,128)(2,1)} %cache_hbm.1, bf16[512,4096]{1,0:T(8,128)(2,1)} %weight_hbm.1, ...), custom_call_target="tpu_custom_call" | custom-call | flops 1 | bytes 1 | tf_op jit(solution)/shard_map/pallas_call | solution.py:99
  20.6 4.1 %all-to-all-done.refs_0_ = bf16[8,32,1920]{2,1,0:T(8,128)(2,1)S(1)} async-done(((bf16[8,32,1920]{2,1,0:T(8,128)(2,1)}), bf16[8,32,1920]{2,1,0:T(8,128)(2,1)S(1)}, u32[]{:S(2)}, u32[]{:S(2)}) %all-to-all-start) | async-done | bytes 983072 | tf_op jit(solution)/shard_map/over_t/all_to_all | solution.py:192
  24.7 0.8 collective-permute-start.4
  25.5 1.2 %collective-permute-start.2 = (bf16[8,32,1920]{2,1,0:T(8,128)(2,1)S(1)}, bf16[8,32,1920]{2,1,0:T(8,128)(2,1)S(1)}, u32[]{:S(2)}, u32[]{:S(2)}) collective-permute-start(bf16[8,32,1920]{2,1,0:T(8,128)(2,1)S(1)} %get-tuple-element.17.refs_0_), channel_id=1, source_target_pairs={{0,16},{1,17},{2,18},{3,19},{8,24},{9,25},{10,26},{11,27},{16,32},... | collective-permute-start | bytes 2949128 | tf_op jit(solution)/shard_map/own_x/ppermute | solution.py:22
  26.8 1.5 %collective-permute-start.3 = (bf16[8,32,1920]{2,1,0:T(8,128)(2,1)S(1)}, bf16[8,32,1920]{2,1,0:T(8,128)(2,1)}, u32[]{:S(2)}, u32[]{:S(2)}) collective-permute-start(bf16[8,32,1920]{2,1,0:T(8,128)(2,1)S(1)} %get-tuple-element.17.refs_0_), channel_id=1, source_target_pairs={{0,48},{1,49},{2,50},{3,51},{8,56},{9,57},{10,58},{11,59},{16,0},{... | collective-permute-start | bytes 2949128 | tf_op jit(solution)/shard_map/own_x/ppermute | solution.py:22
  28.2 3.5 %all-to-all-start.1 = ((f32[4,2,64,512]{3,2,1,0:T(8,128)}), f32[4,2,64,512]{3,2,1,0:T(8,128)S(1)}, u32[]{:S(2)}, u32[]{:S(2)}) async-start(f32[4,2,64,512]{3,2,1,0:T(8,128)} %get-tuple-element.18), calls=%async_computation.1 | async-start | bytes 2097152 | tf_op jit(solution)/shard_map/sum_y/all_to_all | solution.py:202
  31.7 3.4 %collective-permute-start = (bf16[8,32,1920]{2,1,0:T(8,128)(2,1)S(1)}, bf16[8,32,1920]{2,1,0:T(8,128)(2,1)}, u32[]{:S(2)}, u32[]{:S(2)}) collective-permute-start(bf16[8,32,1920]{2,1,0:T(8,128)(2,1)S(1)} %get-tuple-element.17.refs_0_), channel_id=1, source_target_pairs={{0,64},{1,65},{2,66},{3,67},{8,72},{9,73},{10,74},{11,75},{16,80},... | collective-permute-start | bytes 2949128 | tf_op jit(solution)/shard_map/over_z/ppermute | solution.py:22
  35.2 2.5 %shard_map.80.refs_3_ = bf16[2,4,2,8,32,1920]{5,4,3,2,1,0:T(8,128)(2,1)} custom-call(s32[6]{0:T(128)S(1)} %stack.35.index_ref, bf16[8,32,1920]{2,1,0:T(8,128)(2,1)S(1)} %get-tuple-element.17.refs_0_, bf16[8,32,1920]{2,1,0:T(8,128)(2,1)} %collective-permute-done.4.refs_1_), custom_call_target="tpu_custom_call" | custom-call | tf_op jit(solution)/shard_map/pallas_call | solution.py:147
  37.7 8.7 %all-to-all-done.1.refs_2_ = f32[4,2,64,512]{3,2,1,0:T(8,128)S(1)} async-done(((f32[4,2,64,512]{3,2,1,0:T(8,128)}), f32[4,2,64,512]{3,2,1,0:T(8,128)S(1)}, u32[]{:S(2)}, u32[]{:S(2)}) %all-to-all-start.1) | async-done | bytes 1048608 | tf_op jit(solution)/shard_map/sum_y/all_to_all | solution.py:202
  46.4 3.8 %collective-permute-done.2.refs_0_ = bf16[8,32,1920]{2,1,0:T(8,128)(2,1)S(1)} collective-permute-done((bf16[8,32,1920]{2,1,0:T(8,128)(2,1)S(1)}, bf16[8,32,1920]{2,1,0:T(8,128)(2,1)S(1)}, u32[]{:S(2)}, u32[]{:S(2)}) %collective-permute-start.2) | collective-permute-done | bytes 983072 | tf_op jit(solution)/shard_map/own_x/ppermute | solution.py:22
  52.3 1.9 %slice.7 = bf16[4,32,1920]{2,1,0:T(8,128)(2,1)} slice(bf16[8,32,1920]{2,1,0:T(8,128)(2,1)} %get-tuple-element.20.refs_2_), slice={[4:8], [0:32], [0:1920]} | slice | bytes 983040 | tf_op jit(solution)/shard_map/own_x2/slice | solution.py:210
  54.2 1.2 %collective-permute-start.5 = (bf16[4,32,1920]{2,1,0:T(8,128)(2,1)}, bf16[4,32,1920]{2,1,0:T(8,128)(2,1)S(1)}, u32[]{:S(2)}, u32[]{:S(2)}) collective-permute-start(bf16[4,32,1920]{2,1,0:T(8,128)(2,1)} %slice.6), channel_id=1, source_target_pairs={{0,16},{1,17},{2,18},{3,19},{8,24},{9,25},{10,26},{11,27},{16,32},... | collective-permute-start | bytes 1474568 | tf_op jit(solution)/shard_map/own_x2/ppermute | solution.py:22
  55.4 1.4 %collective-permute-done.refs_0_ = bf16[8,32,1920]{2,1,0:T(8,128)(2,1)} collective-permute-done((bf16[8,32,1920]{2,1,0:T(8,128)(2,1)S(1)}, bf16[8,32,1920]{2,1,0:T(8,128)(2,1)}, u32[]{:S(2)}, u32[]{:S(2)}) %collective-permute-start) | collective-permute-done | bytes 983072 | tf_op jit(solution)/shard_map/over_z/ppermute | solution.py:22
  56.8 1.3 %collective-permute-start.6 = (bf16[4,32,1920]{2,1,0:T(8,128)(2,1)}, bf16[4,32,1920]{2,1,0:T(8,128)(2,1)}, u32[]{:S(2)}, u32[]{:S(2)}) collective-permute-start(bf16[4,32,1920]{2,1,0:T(8,128)(2,1)} %slice.7), channel_id=1, source_target_pairs={{0,48},{1,49},{2,50},{3,51},{8,56},{9,57},{10,58},{11,59},{16,0},{... | collective-permute-start | bytes 1474568 | tf_op jit(solution)/shard_map/own_x2/ppermute | solution.py:22
  58.9 1.4 %collective-permute-start.13 = (bf16[8,32,1920]{2,1,0:T(8,128)(2,1)}, bf16[8,32,1920]{2,1,0:T(8,128)(2,1)}, u32[]{:S(2)}, u32[]{:S(2)}) collective-permute-start(bf16[8,32,1920]{2,1,0:T(8,128)(2,1)} %collective-permute-done.refs_0_), channel_id=1, source_target_pairs={{0,8},{1,9},{2,10},{3,11},{8,0},{9,1},{10,2},{11,3},{16,24},{17,25... | collective-permute-start | bytes 2949128 | tf_op jit(solution)/shard_map/core/ppermute | solution.py:22
  61.2 2.6 %collective-permute-start.12 = (bf16[8,32,1920]{2,1,0:T(8,128)(2,1)}, bf16[8,32,1920]{2,1,0:T(8,128)(2,1)S(1)}, u32[]{:S(2)}, u32[]{:S(2)}) collective-permute-start(bf16[8,32,1920]{2,1,0:T(8,128)(2,1)} %collective-permute-done.refs_0_), channel_id=1, source_target_pairs={{0,48},{1,49},{2,50},{3,51},{8,56},{9,57},{10,58},{11,59},{16,0},{... | collective-permute-start | bytes 2949128 | tf_op jit(solution)/shard_map/dup_x/ppermute | solution.py:22
  63.7 3.8 %shard_map.82.refs_3_ = bf16[2,4,2,8,32,1920]{5,4,3,2,1,0:T(8,128)(2,1)} custom-call(s32[12]{0:T(128)S(1)} %stack.36.index_ref, bf16[8,32,1920]{2,1,0:T(8,128)(2,1)S(1)} %get-tuple-element.19.refs_0_, bf16[8,32,1920]{2,1,0:T(8,128)(2,1)} %collective-permute-done.8.refs_1_, ...), custom_call_target="tpu_custom_call", output_to_operand_aliasing={{}: (5, {})} | custom-call | tf_op jit(solution)/shard_map/pallas_call | solution.py:147
  68.1 5.1 %collective-permute-start.14 = (bf16[4,32,1920]{2,1,0:T(8,128)(2,1)S(1)}, bf16[4,32,1920]{2,1,0:T(8,128)(2,1)S(1)}, u32[]{:S(2)}, u32[]{:S(2)}) collective-permute-start(bf16[4,32,1920]{2,1,0:T(8,128)(2,1)S(1)} %get-tuple-element.23.refs_2_), channel_id=1, source_target_pairs={{0,8},{1,9},{2,10},{3,11},{8,0},{9,1},{10,2},{11,3},{16,24},{17,25... | collective-permute-start | bytes 1474568 | tf_op jit(solution)/shard_map/core/ppermute | solution.py:22
  73.1 3.3 %collective-permute-start.10 = (bf16[4,32,1920]{2,1,0:T(8,128)(2,1)S(1)}, bf16[4,32,1920]{2,1,0:T(8,128)(2,1)S(1)}, u32[]{:S(2)}, u32[]{:S(2)}) collective-permute-start(bf16[4,32,1920]{2,1,0:T(8,128)(2,1)S(1)} %get-tuple-element.23.refs_2_), channel_id=1, source_target_pairs={{0,64},{1,65},{2,66},{3,67},{8,72},{9,73},{10,74},{11,75},{16,80},... | collective-permute-start | bytes 1474568 | tf_op jit(solution)/shard_map/over_z2/ppermute | solution.py:22
  77.2 2.1 %collective-permute-start.11 = (bf16[4,32,1920]{2,1,0:T(8,128)(2,1)}, bf16[4,32,1920]{2,1,0:T(8,128)(2,1)S(1)}, u32[]{:S(2)}, u32[]{:S(2)}) collective-permute-start(bf16[4,32,1920]{2,1,0:T(8,128)(2,1)} %get-tuple-element.24.refs_4_), channel_id=1, source_target_pairs={{0,64},{1,65},{2,66},{3,67},{8,72},{9,73},{10,74},{11,75},{16,80},... | collective-permute-start | bytes 1474568 | tf_op jit(solution)/shard_map/over_z2/ppermute | solution.py:22
  79.5 1.0 copy-done.2
  80.5 3.7 %shard_map.84.refs_4_ = bf16[2,4,2,8,32,1920]{5,4,3,2,1,0:T(8,128)(2,1)} custom-call(s32[18]{0:T(128)S(1)} %stack.37.index_ref, bf16[8,32,1920]{2,1,0:T(8,128)(2,1)} %collective-permute-done.refs_0_, bf16[8,32,1920]{2,1,0:T(8,128)(2,1)} %collective-permute-done.13.refs_1_, ...), custom_call_target="tpu_custom_call", output_to_operand_aliasing={{}: (7, {})} | custom-call | tf_op jit(solution)/shard_map/pallas_call | solution.py:147
  84.2 4.4 %collective-permute-done.1.refs_0_ = bf16[8,32,1920]{2,1,0:T(8,128)(2,1)S(1)} collective-permute-done((bf16[8,32,1920]{2,1,0:T(8,128)(2,1)}, bf16[8,32,1920]{2,1,0:T(8,128)(2,1)S(1)}, u32[]{:S(2)}, u32[]{:S(2)}) %collective-permute-start.1) | collective-permute-done | bytes 983072 | tf_op jit(solution)/shard_map/dup_x/ppermute | solution.py:22
  89.0 9.0 %collective-permute-done.11.refs_2_ = bf16[4,32,1920]{2,1,0:T(8,128)(2,1)S(1)} collective-permute-done((bf16[4,32,1920]{2,1,0:T(8,128)(2,1)}, bf16[4,32,1920]{2,1,0:T(8,128)(2,1)S(1)}, u32[]{:S(2)}, u32[]{:S(2)}) %collective-permute-start.11) | collective-permute-done | bytes 491552 | tf_op jit(solution)/shard_map/over_z2/ppermute | solution.py:22
  98.1 1.0 collective-permute-start.16
  99.8 2.2 %shard_map.86.refs_4_ = bf16[2,4,2,8,32,1920]{5,4,3,2,1,0:T(8,128)(2,1)} custom-call(s32[12]{0:T(128)S(1)} %stack.38.index_ref, bf16[8,32,1920]{2,1,0:T(8,128)(2,1)S(1)} %get-tuple-element.26.refs_0_, bf16[8,32,1920]{2,1,0:T(8,128)(2,1)S(1)} %get-tuple-element.27.refs_1_, ...), custom_call_target="tpu_custom_call", output_to_operand_aliasing={{}: (5, {})} | custom-call | tf_op jit(solution)/shard_map/pallas_call | solution.py:147
  102.7 1.5 %collective-permute-done.19.refs_3_ = bf16[4,32,1920]{2,1,0:T(8,128)(2,1)} collective-permute-done((bf16[4,32,1920]{2,1,0:T(8,128)(2,1)S(1)}, bf16[4,32,1920]{2,1,0:T(8,128)(2,1)}, u32[]{:S(2)}, u32[]{:S(2)}) %collective-permute-start.19) | collective-permute-done | bytes 491552 | tf_op jit(solution)/shard_map/core/ppermute | solution.py:22
  104.3 3.3 %shard_map.87 = bf16[2,4,2,8,32,1920]{5,4,3,2,1,0:T(8,128)(2,1)} custom-call(s32[12]{0:T(128)S(1)} %stack.31.index_ref, bf16[8,32,1920]{2,1,0:T(8,128)(2,1)} %collective-permute-done.16.refs_0_, bf16[8,32,1920]{2,1,0:T(8,128)(2,1)} %collective-permute-done.17.refs_1_, ...), custom_call_target="tpu_custom_call", output_to_operand_aliasing={{}: (5, {})} | custom-call | tf_op jit(solution)/shard_map/pallas_call | solution.py:147
  (45 shorter events, 8.4 us)
Async XLA Ops:
  0.6 1.5 %copy-start = (f32[32,15360]{1,0:T(8,128)S(1)}, f32[32,15360]{1,0:T(8,128)}, u32[]{:S(2)}) copy-start(f32[32,15360]{1,0:T(8,128)} %in_ref.1) | copy-start | bytes 5898244
  3.2 21.5 %all-to-all-start = ((bf16[8,32,1920]{2,1,0:T(8,128)(2,1)}), bf16[8,32,1920]{2,1,0:T(8,128)(2,1)S(1)}, u32[]{:S(2)}, u32[]{:S(2)}) async-start(bf16[8,32,1920]{2,1,0:T(8,128)(2,1)} %shard_map.77.after_ref), calls=%async_computation | async-start | bytes 1966080 | tf_op jit(solution)/shard_map/over_t/all_to_all | solution.py:192
  9.6 0.8 copy-start.3
  10.4 0.8 copy-start.4
  11.2 0.7 copy-start.5
  24.7 10.5 %collective-permute-start.4 = (bf16[8,32,1920]{2,1,0:T(8,128)(2,1)S(1)}, bf16[8,32,1920]{2,1,0:T(8,128)(2,1)}, u32[]{:S(2)}, u32[]{:S(2)}) collective-permute-start(bf16[8,32,1920]{2,1,0:T(8,128)(2,1)S(1)} %get-tuple-element.17.refs_0_), channel_id=1, source_target_pairs={{0,8},{1,9},{2,10},{3,11},{8,0},{9,1},{10,2},{11,3},{16,24},{17,25... | collective-permute-start | bytes 2949128 | tf_op jit(solution)/shard_map/core/ppermute | solution.py:22
  25.5 24.7 %collective-permute-start.2 = (bf16[8,32,1920]{2,1,0:T(8,128)(2,1)S(1)}, bf16[8,32,1920]{2,1,0:T(8,128)(2,1)S(1)}, u32[]{:S(2)}, u32[]{:S(2)}) collective-permute-start(bf16[8,32,1920]{2,1,0:T(8,128)(2,1)S(1)} %get-tuple-element.17.refs_0_), channel_id=1, source_target_pairs={{0,16},{1,17},{2,18},{3,19},{8,24},{9,25},{10,26},{11,27},{16,32},... | collective-permute-start | bytes 2949128 | tf_op jit(solution)/shard_map/own_x/ppermute | solution.py:22
  26.8 23.5 %collective-permute-start.3 = (bf16[8,32,1920]{2,1,0:T(8,128)(2,1)S(1)}, bf16[8,32,1920]{2,1,0:T(8,128)(2,1)}, u32[]{:S(2)}, u32[]{:S(2)}) collective-permute-start(bf16[8,32,1920]{2,1,0:T(8,128)(2,1)S(1)} %get-tuple-element.17.refs_0_), channel_id=1, source_target_pairs={{0,48},{1,49},{2,50},{3,51},{8,56},{9,57},{10,58},{11,59},{16,0},{... | collective-permute-start | bytes 2949128 | tf_op jit(solution)/shard_map/own_x/ppermute | solution.py:22
  28.2 18.2 %all-to-all-start.1 = ((f32[4,2,64,512]{3,2,1,0:T(8,128)}), f32[4,2,64,512]{3,2,1,0:T(8,128)S(1)}, u32[]{:S(2)}, u32[]{:S(2)}) async-start(f32[4,2,64,512]{3,2,1,0:T(8,128)} %get-tuple-element.18), calls=%async_computation.1 | async-start | bytes 2097152 | tf_op jit(solution)/shard_map/sum_y/all_to_all | solution.py:202
  31.7 25.1 %collective-permute-start = (bf16[8,32,1920]{2,1,0:T(8,128)(2,1)S(1)}, bf16[8,32,1920]{2,1,0:T(8,128)(2,1)}, u32[]{:S(2)}, u32[]{:S(2)}) collective-permute-start(bf16[8,32,1920]{2,1,0:T(8,128)(2,1)S(1)} %get-tuple-element.17.refs_0_), channel_id=1, source_target_pairs={{0,64},{1,65},{2,66},{3,67},{8,72},{9,73},{10,74},{11,75},{16,80},... | collective-permute-start | bytes 2949128 | tf_op jit(solution)/shard_map/over_z/ppermute | solution.py:22
  50.3 10.8 %collective-permute-start.8 = (bf16[8,32,1920]{2,1,0:T(8,128)(2,1)S(1)}, bf16[8,32,1920]{2,1,0:T(8,128)(2,1)}, u32[]{:S(2)}, u32[]{:S(2)}) collective-permute-start(bf16[8,32,1920]{2,1,0:T(8,128)(2,1)S(1)} %get-tuple-element.19.refs_0_), channel_id=1, source_target_pairs={{0,8},{1,9},{2,10},{3,11},{8,0},{9,1},{10,2},{11,3},{16,24},{17,25... | collective-permute-start | bytes 2949128 | tf_op jit(solution)/shard_map/core/ppermute | solution.py:22
  51.0 10.1 %collective-permute-start.9 = (bf16[8,32,1920]{2,1,0:T(8,128)(2,1)}, bf16[8,32,1920]{2,1,0:T(8,128)(2,1)}, u32[]{:S(2)}, u32[]{:S(2)}) collective-permute-start(bf16[8,32,1920]{2,1,0:T(8,128)(2,1)} %get-tuple-element.20.refs_2_), channel_id=1, source_target_pairs={{0,8},{1,9},{2,10},{3,11},{8,0},{9,1},{10,2},{11,3},{16,24},{17,25... | collective-permute-start | bytes 2949128 | tf_op jit(solution)/shard_map/core/ppermute | solution.py:22
  51.2 7.7 %collective-permute-start.7 = (f32[64,512]{1,0:T(8,128)S(1)}, f32[64,512]{1,0:T(8,128)S(1)}, u32[]{:S(2)}, u32[]{:S(2)}) collective-permute-start(f32[64,512]{1,0:T(8,128)S(1)} %dynamic-slice_bitcast_fusion), channel_id=1, source_target_pairs={{0,4},{1,5},{2,6},{3,7},{4,0},{5,1},{6,2},{7,3},{8,12},{9,13},{10,... | collective-permute-start | bytes 393224 | tf_op jit(solution)/shard_map/sum_z/ppermute | solution.py:216
  54.2 13.4 %collective-permute-start.5 = (bf16[4,32,1920]{2,1,0:T(8,128)(2,1)}, bf16[4,32,1920]{2,1,0:T(8,128)(2,1)S(1)}, u32[]{:S(2)}, u32[]{:S(2)}) collective-permute-start(bf16[4,32,1920]{2,1,0:T(8,128)(2,1)} %slice.6), channel_id=1, source_target_pairs={{0,16},{1,17},{2,18},{3,19},{8,24},{9,25},{10,26},{11,27},{16,32},... | collective-permute-start | bytes 1474568 | tf_op jit(solution)/shard_map/own_x2/ppermute | solution.py:22
  56.8 11.2 %collective-permute-start.6 = (bf16[4,32,1920]{2,1,0:T(8,128)(2,1)}, bf16[4,32,1920]{2,1,0:T(8,128)(2,1)}, u32[]{:S(2)}, u32[]{:S(2)}) collective-permute-start(bf16[4,32,1920]{2,1,0:T(8,128)(2,1)} %slice.7), channel_id=1, source_target_pairs={{0,48},{1,49},{2,50},{3,51},{8,56},{9,57},{10,58},{11,59},{16,0},{... | collective-permute-start | bytes 1474568 | tf_op jit(solution)/shard_map/own_x2/ppermute | solution.py:22
  58.9 14.2 %collective-permute-start.13 = (bf16[8,32,1920]{2,1,0:T(8,128)(2,1)}, bf16[8,32,1920]{2,1,0:T(8,128)(2,1)}, u32[]{:S(2)}, u32[]{:S(2)}) collective-permute-start(bf16[8,32,1920]{2,1,0:T(8,128)(2,1)} %collective-permute-done.refs_0_), channel_id=1, source_target_pairs={{0,8},{1,9},{2,10},{3,11},{8,0},{9,1},{10,2},{11,3},{16,24},{17,25... | collective-permute-start | bytes 2949128 | tf_op jit(solution)/shard_map/core/ppermute | solution.py:22
  61.1 27.6 %collective-permute-start.1 = (bf16[8,32,1920]{2,1,0:T(8,128)(2,1)}, bf16[8,32,1920]{2,1,0:T(8,128)(2,1)S(1)}, u32[]{:S(2)}, u32[]{:S(2)}) collective-permute-start(bf16[8,32,1920]{2,1,0:T(8,128)(2,1)} %collective-permute-done.refs_0_), channel_id=1, source_target_pairs={{0,16},{1,17},{2,18},{3,19},{8,24},{9,25},{10,26},{11,27},{16,32},... | collective-permute-start | bytes 2949128 | tf_op jit(solution)/shard_map/dup_x/ppermute | solution.py:22
  61.2 27.9 %collective-permute-start.12 = (bf16[8,32,1920]{2,1,0:T(8,128)(2,1)}, bf16[8,32,1920]{2,1,0:T(8,128)(2,1)S(1)}, u32[]{:S(2)}, u32[]{:S(2)}) collective-permute-start(bf16[8,32,1920]{2,1,0:T(8,128)(2,1)} %collective-permute-done.refs_0_), channel_id=1, source_target_pairs={{0,48},{1,49},{2,50},{3,51},{8,56},{9,57},{10,58},{11,59},{16,0},{... | collective-permute-start | bytes 2949128 | tf_op jit(solution)/shard_map/dup_x/ppermute | solution.py:22
  68.1 8.3 %collective-permute-start.14 = (bf16[4,32,1920]{2,1,0:T(8,128)(2,1)S(1)}, bf16[4,32,1920]{2,1,0:T(8,128)(2,1)S(1)}, u32[]{:S(2)}, u32[]{:S(2)}) collective-permute-start(bf16[4,32,1920]{2,1,0:T(8,128)(2,1)S(1)} %get-tuple-element.23.refs_2_), channel_id=1, source_target_pairs={{0,8},{1,9},{2,10},{3,11},{8,0},{9,1},{10,2},{11,3},{16,24},{17,25... | collective-permute-start | bytes 1474568 | tf_op jit(solution)/shard_map/core/ppermute | solution.py:22
  73.1 6.3 %collective-permute-start.15 = (bf16[4,32,1920]{2,1,0:T(8,128)(2,1)}, bf16[4,32,1920]{2,1,0:T(8,128)(2,1)}, u32[]{:S(2)}, u32[]{:S(2)}) collective-permute-start(bf16[4,32,1920]{2,1,0:T(8,128)(2,1)} %get-tuple-element.24.refs_4_), channel_id=1, source_target_pairs={{0,8},{1,9},{2,10},{3,11},{8,0},{9,1},{10,2},{11,3},{16,24},{17,25... | collective-permute-start | bytes 1474568 | tf_op jit(solution)/shard_map/core/ppermute | solution.py:22
  73.1 15.9 %collective-permute-start.10 = (bf16[4,32,1920]{2,1,0:T(8,128)(2,1)S(1)}, bf16[4,32,1920]{2,1,0:T(8,128)(2,1)S(1)}, u32[]{:S(2)}, u32[]{:S(2)}) collective-permute-start(bf16[4,32,1920]{2,1,0:T(8,128)(2,1)S(1)} %get-tuple-element.23.refs_2_), channel_id=1, source_target_pairs={{0,64},{1,65},{2,66},{3,67},{8,72},{9,73},{10,74},{11,75},{16,80},... | collective-permute-start | bytes 1474568 | tf_op jit(solution)/shard_map/over_z2/ppermute | solution.py:22
  76.4 0.8 copy-start.1
  77.2 20.9 %collective-permute-start.11 = (bf16[4,32,1920]{2,1,0:T(8,128)(2,1)}, bf16[4,32,1920]{2,1,0:T(8,128)(2,1)S(1)}, u32[]{:S(2)}, u32[]{:S(2)}) collective-permute-start(bf16[4,32,1920]{2,1,0:T(8,128)(2,1)} %get-tuple-element.24.refs_4_), channel_id=1, source_target_pairs={{0,64},{1,65},{2,66},{3,67},{8,72},{9,73},{10,74},{11,75},{16,80},... | collective-permute-start | bytes 1474568 | tf_op jit(solution)/shard_map/over_z2/ppermute | solution.py:22
  79.4 1.0 copy-start.2
  98.1 6.2 %collective-permute-start.16 = (bf16[8,32,1920]{2,1,0:T(8,128)(2,1)S(1)}, bf16[8,32,1920]{2,1,0:T(8,128)(2,1)}, u32[]{:S(2)}, u32[]{:S(2)}) collective-permute-start(bf16[8,32,1920]{2,1,0:T(8,128)(2,1)S(1)} %get-tuple-element.26.refs_0_), channel_id=1, source_target_pairs={{0,8},{1,9},{2,10},{3,11},{8,0},{9,1},{10,2},{11,3},{16,24},{17,25... | collective-permute-start | bytes 2949128 | tf_op jit(solution)/shard_map/core/ppermute | solution.py:22
  99.1 5.1 %collective-permute-start.17 = (bf16[8,32,1920]{2,1,0:T(8,128)(2,1)S(1)}, bf16[8,32,1920]{2,1,0:T(8,128)(2,1)}, u32[]{:S(2)}, u32[]{:S(2)}) collective-permute-start(bf16[8,32,1920]{2,1,0:T(8,128)(2,1)S(1)} %get-tuple-element.27.refs_1_), channel_id=1, source_target_pairs={{0,8},{1,9},{2,10},{3,11},{8,0},{9,1},{10,2},{11,3},{16,24},{17,25... | collective-permute-start | bytes 2949128 | tf_op jit(solution)/shard_map/core/ppermute | solution.py:22
  99.1 3.6 %collective-permute-start.18 = (bf16[4,32,1920]{2,1,0:T(8,128)(2,1)S(1)}, bf16[4,32,1920]{2,1,0:T(8,128)(2,1)S(1)}, u32[]{:S(2)}, u32[]{:S(2)}) collective-permute-start(bf16[4,32,1920]{2,1,0:T(8,128)(2,1)S(1)} %get-tuple-element.28.refs_2_), channel_id=1, source_target_pairs={{0,8},{1,9},{2,10},{3,11},{8,0},{9,1},{10,2},{11,3},{16,24},{17,25... | collective-permute-start | bytes 1474568 | tf_op jit(solution)/shard_map/core/ppermute | solution.py:22
  99.6 4.6 %collective-permute-start.19 = (bf16[4,32,1920]{2,1,0:T(8,128)(2,1)S(1)}, bf16[4,32,1920]{2,1,0:T(8,128)(2,1)}, u32[]{:S(2)}, u32[]{:S(2)}) collective-permute-start(bf16[4,32,1920]{2,1,0:T(8,128)(2,1)S(1)} %get-tuple-element.29.refs_3_), channel_id=1, source_target_pairs={{0,8},{1,9},{2,10},{3,11},{8,0},{9,1},{10,2},{11,3},{16,24},{17,25... | collective-permute-start | bytes 1474568 | tf_op jit(solution)/shard_map/core/ppermute | solution.py:22

commit v2 on v1

--- a/solution.py
+++ b/solution.py
@@ -155,7 +155,7 @@
     )(*operands)
 
 
-def fence(*values):
+def fence(*values, cost=0):
     def kernel(*refs):
         pass
 
@@ -166,6 +166,7 @@
         out_shape=[jax.ShapeDtypeStruct(v.shape, v.dtype) for v in values],
         input_output_aliases={k: k for k in range(len(values))},
         compiler_params=pltpu.CompilerParams(vmem_limit_bytes=1 << 20),
+        cost_estimate=pl.CostEstimate(flops=0, bytes_accessed=cost, transcendentals=0),
     )(*values)
     return made if len(values) > 1 else made[0]
 
@@ -206,27 +207,36 @@
     out = place(None, both(own, z_hi, 0))
     own_1, own_3, shares, out = fence(own_1, own_3, shares, out)
 
+    low_1, high_3 = own_1[:4], own_3[4:]
     with jax.named_scope("own_x2"):
-        own_2, own_2b = send(own_1[:4], dx=1), send(own_3[4:], dx=-1)
+        low_2, high_2 = send(low_1, dx=1), send(high_3, dx=-1)
+    with jax.named_scope("dup_z"):
+        dup_low_1 = send(low_1, dz=2)
     with jax.named_scope("dup_x"):
-        dup_1, dup_3 = send(dup, dx=1), send(dup, dx=-1)
-    with jax.named_scope("sum_z"):
-        total = jnp.sum(shares, axis=0)
-        pairs = [(i, i // 8 * 8 + (i + 4) % 8) for i in range(128)]
-        attn = pick(total, z_lo) + lax.ppermute(pick(total, 1 - z_lo), AXES, pairs)
-        attn = attn.astype(jnp.bfloat16)
+        dup_high_1, dup_3 = send(dup[4:], dx=1), send(dup, dx=-1)
+        dup_high_1 = fence(dup_high_1, cost=1 << 20)
     out = place(out, both(own_1, z_hi, 1) + both(own_3, z_hi, 3))
-    own_2, own_2b, attn, out = fence(own_2, own_2b, attn, out)
-
-    with jax.named_scope("over_z2"):
-        dup_2, dup_2b = send(own_2, dz=2), send(own_2b, dz=2)
-    out = place(out, both(dup, 1 - z_hi, 0) + both(own_2, z_hi, 2) + both(own_2b, z_hi, 2, 4))
-    dup_1, dup_2, dup_2b, dup_3, out = fence(dup_1, dup_2, dup_2b, dup_3, out)
-
-    pairs = [both(dup_1, 1 - z_hi, 1), both(dup_3, 1 - z_hi, 3)]
-    pairs += [both(dup_2, 1 - z_hi, 2), both(dup_2b, 1 - z_hi, 2, 4)]
+    low_2, high_2, dup_low_1, shares, out = fence(low_2, high_2, dup_low_1, shares, out)
+
+    with jax.named_scope("dup_x2"):
+        dup_low_2 = send(dup_low_1, dx=1)
+    with jax.named_scope("dup_z2"):
+        dup_high_2 = send(high_2, dz=2)
+    total = jnp.sum(shares, axis=0)
+    kept, given = pick(total, z_lo), pick(total, 1 - z_lo)
+    out = place(out, both(dup, 1 - z_hi, 0) + both(low_2, z_hi, 2) + both(high_2, z_hi, 2, 4))
+    out = place(out, both(dup_low_1, 1 - z_hi, 1))
+    dup_high_1, dup_3, dup_low_2, dup_high_2, kept, given, out = fence(
+        dup_high_1, dup_3, dup_low_2, dup_high_2, kept, given, out
+    )
+
+    pairs = [both(dup_high_1, 1 - z_hi, 1, 4), both(dup_3, 1 - z_hi, 3)]
+    pairs += [both(dup_low_2, 1 - z_hi, 2), both(dup_high_2, 1 - z_hi, 2, 4)]
     out = place(out, [mine for mine, _ in pairs])
     out = place(out, [theirs for _, theirs in pairs])
+    with jax.named_scope("sum_z"):
+        attn = kept + lax.ppermute(given, AXES, [(i, i ^ 4) for i in range(128)])
+        attn = attn.astype(jnp.bfloat16)
     return (out.reshape(-1, width), attn.reshape(r, s, -1))
 
 

time: 108 us -> 105 us (0.972)
  waiting for transfers between devices: 35.5 us -> 27.3 us
  local copies, waits for them, and re-layouts: 8.73 us -> 13 us
  Pallas kernels: 25.2 us -> 27 us
  starting transfers between devices: 36.5 us -> 34.8 us
    ppermute x19 -> x21, waiting for transfers between devices: 21.9 us -> 12.7 us  [send(): return lax.ppermute(value, AXES, pairs)]
    unnamed x12 -> x16, local copies, waits for them, and re-layouts: 5.58 us -> 7.75 us
    pallas_call x5 -> x6, Pallas kernels: 15.4 us -> 17.2 us  [place(): pl.pallas_call(kernel, in_specs=specs, out_specs=pl.BlockSpec(memory_spac...]
    ppermute x19 -> x21, starting transfers between devices: 26.3 us -> 24.9 us  [send(): return lax.ppermute(value, AXES, pairs)]
    slice x2 -> x3, local copies, waits for them, and re-layouts: 2.69 us -> 3.77 us  [the longest x2 2.7 us: local(): low_1, high_3 = (own_1[:4], own_3[4:])]
  transfers between devices with their start and end apart: 22 -> 24, of which waited for: 12 -> 8; matrix products, arithmetic and copies ran while one was open for 4% -> 6% of each run, Pallas kernels for 19% -> 22%
where the time goes in v2:
time: 105 us; the launch traced here: 104 us
  starting transfers between devices  34.8 us (33%)
  waiting for transfers between devices  27.3 us (26%)
  Pallas kernels  27 us (26%)
  local copies, waits for them, and re-layouts  13 us (12%)
  other arithmetic  1.44 us (1%)
    ppermute x21, starting transfers between devices, send(): return lax.ppermute(value, AXES, pairs)  24.9 us
    pallas_call x6, Pallas kernels, place(): pl.pallas_call(kernel, in_specs=specs, out_specs=pl.BlockSpec(memory_spac...  17.2 us
    ppermute x21, waiting for transfers between devices, send(): return lax.ppermute(value, AXES, pairs)  12.7 us
    pallas_call x1, Pallas kernels, attend(): pl.pallas_call(kernel, in_specs=[pl.BlockSpec(memory_space=pltpu.SMEM), v...  8.8 us
    all_to_all x1, waiting for transfers between devices, local(): lax.all_to_all(shares, 'tp', split_axis=0, concat_axis=0, tiled=True, axi...  8.72 us
    unnamed x16, local copies, waits for them, and re-layouts  7.75 us
    all_to_all x1, starting transfers between devices, local(): own = lax.all_to_all(blocks, 'tp', split_axis=0, concat_axis=0, tiled=True)  6.37 us
    all_to_all x1, waiting for transfers between devices, local(): own = lax.all_to_all(blocks, 'tp', split_axis=0, concat_axis=0, tiled=True)  4.05 us
  transfers between devices with their start and end apart: 24, of which 8 were waited for; matrix products, arithmetic and copies ran while one was open for 6% of the time, Pallas kernels for 22%

profile of v2, /device:TPU:1, one launch (start us, length us, event | category | flops | bytes accessed | tf_op | source)
XLA Modules:
  0.0 104.5 jit_solution(2180142557636932129)
XLA Ops:
  0.6 1.5 %copy-done = f32[32,15360]{1,0:T(8,128)S(1)} copy-done((f32[32,15360]{1,0:T(8,128)S(1)}, f32[32,15360]{1,0:T(8,128)}, u32[]{:S(2)}) %copy-start) | copy-done | bytes 1966104
  2.2 1.0 shard_map.77.after_ref
  3.2 6.4 %all-to-all-start = ((bf16[8,32,1920]{2,1,0:T(8,128)(2,1)}), bf16[8,32,1920]{2,1,0:T(8,128)(2,1)S(1)}, u32[]{:S(2)}, u32[]{:S(2)}) async-start(bf16[8,32,1920]{2,1,0:T(8,128)(2,1)} %shard_map.77.after_ref), calls=%async_computation | async-start | bytes 1966080 | tf_op jit(solution)/shard_map/over_t/all_to_all | solution.py:193
  11.8 8.8 %shard_map.78.refs_1_ = f32[4,2,64,512]{3,2,1,0:T(8,128)} custom-call(s32[8]{0:T(128)S(1)} %copy-done.7, bf16[8,8,512]{2,1,0:T(8,128)(2,1)S(1)} %copy-done.5, bf16[8,8,2,128]{3,2,1,0:T(2,128)(2,1)S(1)} %copy-done.6, bf16[8,2,1,1024,128]{4,3,2,1,0:T(8,128)(2,1)} %cache_hbm.1, bf16[512,4096]{1,0:T(8,128)(2,1)} %weight_hbm.1, ...), custom_call_target="tpu_custom_call" | custom-call | flops 1 | bytes 1 | tf_op jit(solution)/shard_map/pallas_call | solution.py:99
  20.6 4.1 %all-to-all-done.refs_0_ = bf16[8,32,1920]{2,1,0:T(8,128)(2,1)S(1)} async-done(((bf16[8,32,1920]{2,1,0:T(8,128)(2,1)}), bf16[8,32,1920]{2,1,0:T(8,128)(2,1)S(1)}, u32[]{:S(2)}, u32[]{:S(2)}) %all-to-all-start) | async-done | bytes 983072 | tf_op jit(solution)/shard_map/over_t/all_to_all | solution.py:193
  25.5 1.2 %collective-permute-start.3 = (bf16[8,32,1920]{2,1,0:T(8,128)(2,1)S(1)}, bf16[8,32,1920]{2,1,0:T(8,128)(2,1)S(1)}, u32[]{:S(2)}, u32[]{:S(2)}) collective-permute-start(bf16[8,32,1920]{2,1,0:T(8,128)(2,1)S(1)} %get-tuple-element.20.refs_0_), channel_id=1, source_target_pairs={{0,16},{1,17},{2,18},{3,19},{8,24},{9,25},{10,26},{11,27},{16,32},... | collective-permute-start | bytes 2949128 | tf_op jit(solution)/shard_map/own_x/ppermute | solution.py:22
  26.8 1.5 %collective-permute-start.4 = (bf16[8,32,1920]{2,1,0:T(8,128)(2,1)S(1)}, bf16[8,32,1920]{2,1,0:T(8,128)(2,1)}, u32[]{:S(2)}, u32[]{:S(2)}) collective-permute-start(bf16[8,32,1920]{2,1,0:T(8,128)(2,1)S(1)} %get-tuple-element.20.refs_0_), channel_id=1, source_target_pairs={{0,48},{1,49},{2,50},{3,51},{8,56},{9,57},{10,58},{11,59},{16,0},{... | collective-permute-start | bytes 2949128 | tf_op jit(solution)/shard_map/own_x/ppermute | solution.py:22
  28.2 3.5 %all-to-all-start.1 = ((f32[4,2,64,512]{3,2,1,0:T(8,128)}), f32[4,2,64,512]{3,2,1,0:T(8,128)S(1)}, u32[]{:S(2)}, u32[]{:S(2)}) async-start(f32[4,2,64,512]{3,2,1,0:T(8,128)} %get-tuple-element.21), calls=%async_computation.1 | async-start | bytes 2097152 | tf_op jit(solution)/shard_map/sum_y/all_to_all | solution.py:203
  31.9 3.3 %collective-permute-start = (bf16[8,32,1920]{2,1,0:T(8,128)(2,1)S(1)}, bf16[8,32,1920]{2,1,0:T(8,128)(2,1)}, u32[]{:S(2)}, u32[]{:S(2)}) collective-permute-start(bf16[8,32,1920]{2,1,0:T(8,128)(2,1)S(1)} %get-tuple-element.20.refs_0_), channel_id=1, source_target_pairs={{0,64},{1,65},{2,66},{3,67},{8,72},{9,73},{10,74},{11,75},{16,80},... | collective-permute-start | bytes 2949128 | tf_op jit(solution)/shard_map/over_z/ppermute | solution.py:22
  35.2 2.5 %shard_map.80.refs_3_ = bf16[2,4,2,8,32,1920]{5,4,3,2,1,0:T(8,128)(2,1)} custom-call(s32[6]{0:T(128)S(1)} %stack.37.index_ref, bf16[8,32,1920]{2,1,0:T(8,128)(2,1)S(1)} %get-tuple-element.20.refs_0_, bf16[8,32,1920]{2,1,0:T(8,128)(2,1)} %collective-permute-done.5.refs_1_), custom_call_target="tpu_custom_call" | custom-call | tf_op jit(solution)/shard_map/pallas_call | solution.py:147
  37.7 8.7 %all-to-all-done.1.refs_2_ = f32[4,2,64,512]{3,2,1,0:T(8,128)S(1)} async-done(((f32[4,2,64,512]{3,2,1,0:T(8,128)}), f32[4,2,64,512]{3,2,1,0:T(8,128)S(1)}, u32[]{:S(2)}, u32[]{:S(2)}) %all-to-all-start.1) | async-done | bytes 1048608 | tf_op jit(solution)/shard_map/sum_y/all_to_all | solution.py:203
  46.4 3.8 %collective-permute-done.3.refs_0_ = bf16[8,32,1920]{2,1,0:T(8,128)(2,1)S(1)} collective-permute-done((bf16[8,32,1920]{2,1,0:T(8,128)(2,1)S(1)}, bf16[8,32,1920]{2,1,0:T(8,128)(2,1)S(1)}, u32[]{:S(2)}, u32[]{:S(2)}) %collective-permute-start.3) | collective-permute-done | bytes 983072 | tf_op jit(solution)/shard_map/own_x/ppermute | solution.py:22
  51.9 1.9 %slice.11 = bf16[4,32,1920]{2,1,0:T(8,128)(2,1)} slice(bf16[8,32,1920]{2,1,0:T(8,128)(2,1)} %get-tuple-element.23.refs_2_), slice={[4:8], [0:32], [0:1920]} | slice | bytes 983040 | tf_op jit(solution)/shard_map/slice | solution.py:210
  53.7 1.2 %collective-permute-start.6 = (bf16[4,32,1920]{2,1,0:T(8,128)(2,1)}, bf16[4,32,1920]{2,1,0:T(8,128)(2,1)S(1)}, u32[]{:S(2)}, u32[]{:S(2)}) collective-permute-start(bf16[4,32,1920]{2,1,0:T(8,128)(2,1)} %slice.10), channel_id=1, source_target_pairs={{0,16},{1,17},{2,18},{3,19},{8,24},{9,25},{10,26},{11,27},{16,32},... | collective-permute-start | bytes 1474568 | tf_op jit(solution)/shard_map/own_x2/ppermute | solution.py:22
  55.0 1.5 %collective-permute-start.7 = (bf16[4,32,1920]{2,1,0:T(8,128)(2,1)}, bf16[4,32,1920]{2,1,0:T(8,128)(2,1)}, u32[]{:S(2)}, u32[]{:S(2)}) collective-permute-start(bf16[4,32,1920]{2,1,0:T(8,128)(2,1)} %slice.11), channel_id=1, source_target_pairs={{0,48},{1,49},{2,50},{3,51},{8,56},{9,57},{10,58},{11,59},{16,0},{... | collective-permute-start | bytes 1474568 | tf_op jit(solution)/shard_map/own_x2/ppermute | solution.py:22
  56.9 2.8 %collective-permute-start.8 = (bf16[4,32,1920]{2,1,0:T(8,128)(2,1)}, bf16[4,32,1920]{2,1,0:T(8,128)(2,1)}, u32[]{:S(2)}, u32[]{:S(2)}) collective-permute-start(bf16[4,32,1920]{2,1,0:T(8,128)(2,1)} %slice.10), channel_id=1, source_target_pairs={{0,64},{1,65},{2,66},{3,67},{8,72},{9,73},{10,74},{11,75},{16,80},... | collective-permute-start | bytes 1474568 | tf_op jit(solution)/shard_map/dup_z/ppermute | solution.py:22
  60.7 1.5 %collective-permute-start.14 = (bf16[8,32,1920]{2,1,0:T(8,128)(2,1)}, bf16[8,32,1920]{2,1,0:T(8,128)(2,1)}, u32[]{:S(2)}, u32[]{:S(2)}) collective-permute-start(bf16[8,32,1920]{2,1,0:T(8,128)(2,1)} %collective-permute-done.refs_0_), channel_id=1, source_target_pairs={{0,8},{1,9},{2,10},{3,11},{8,0},{9,1},{10,2},{11,3},{16,24},{17,25... | collective-permute-start | bytes 2949128 | tf_op jit(solution)/shard_map/core/ppermute | solution.py:22
  62.3 1.1 %slice.12 = bf16[4,32,1920]{2,1,0:T(8,128)(2,1)S(1)} slice(bf16[8,32,1920]{2,1,0:T(8,128)(2,1)} %collective-permute-done.refs_0_), slice={[4:8], [0:32], [0:1920]} | slice | bytes 983040 | tf_op jit(solution)/shard_map/dup_x/slice | solution.py:216
  63.5 1.2 %copy-done.2 = bf16[8,32,1920]{2,1,0:T(8,128)(2,1)S(1)} copy-done((bf16[8,32,1920]{2,1,0:T(8,128)(2,1)S(1)}, bf16[8,32,1920]{2,1,0:T(8,128)(2,1)}, u32[]{:S(2)}) %copy-start.2) | copy-done | bytes 983064
  64.7 3.5 %shard_map.82.refs_4_ = bf16[2,4,2,8,32,1920]{5,4,3,2,1,0:T(8,128)(2,1)} custom-call(s32[12]{0:T(128)S(1)} %stack.38.index_ref, bf16[8,32,1920]{2,1,0:T(8,128)(2,1)S(1)} %get-tuple-element.22.refs_0_, bf16[8,32,1920]{2,1,0:T(8,128)(2,1)} %collective-permute-done.9.refs_1_, ...), custom_call_target="tpu_custom_call", output_to_operand_aliasing={{}: (5, {})} | custom-call | tf_op jit(solution)/shard_map/pallas_call | solution.py:147
  68.2 2.7 %collective-permute-start.2 = (bf16[8,32,1920]{2,1,0:T(8,128)(2,1)}, bf16[8,32,1920]{2,1,0:T(8,128)(2,1)S(1)}, u32[]{:S(2)}, u32[]{:S(2)}) collective-permute-start(bf16[8,32,1920]{2,1,0:T(8,128)(2,1)} %collective-permute-done.refs_0_), channel_id=1, source_target_pairs={{0,48},{1,49},{2,50},{3,51},{8,56},{9,57},{10,58},{11,59},{16,0},{... | collective-permute-start | bytes 2949128 | tf_op jit(solution)/shard_map/dup_x/ppermute | solution.py:22
  70.9 1.5 %collective-permute-start.15 = (bf16[4,32,1920]{2,1,0:T(8,128)(2,1)S(1)}, bf16[4,32,1920]{2,1,0:T(8,128)(2,1)S(1)}, u32[]{:S(2)}, u32[]{:S(2)}) collective-permute-start(bf16[4,32,1920]{2,1,0:T(8,128)(2,1)S(1)} %get-tuple-element.29.refs_2_), channel_id=1, source_target_pairs={{0,8},{1,9},{2,10},{3,11},{8,0},{9,1},{10,2},{11,3},{16,24},{17,25... | collective-permute-start | bytes 1474568 | tf_op jit(solution)/shard_map/core/ppermute | solution.py:22
  72.4 5.6 %collective-permute-done.1.refs_0_ = bf16[4,32,1920]{2,1,0:T(8,128)(2,1)S(1)} collective-permute-done((bf16[4,32,1920]{2,1,0:T(8,128)(2,1)S(1)}, bf16[4,32,1920]{2,1,0:T(8,128)(2,1)S(1)}, u32[]{:S(2)}, u32[]{:S(2)}) %collective-permute-start.1) | collective-permute-done | bytes 491552 | tf_op jit(solution)/shard_map/dup_x/ppermute | solution.py:22
  78.0 1.4 %collective-permute-start.13 = (bf16[4,32,1920]{2,1,0:T(8,128)(2,1)}, bf16[4,32,1920]{2,1,0:T(8,128)(2,1)}, u32[]{:S(2)}, u32[]{:S(2)}) collective-permute-start(bf16[4,32,1920]{2,1,0:T(8,128)(2,1)} %get-tuple-element.26.refs_0_), channel_id=1, source_target_pairs={{0,8},{1,9},{2,10},{3,11},{8,0},{9,1},{10,2},{11,3},{16,24},{17,25... | collective-permute-start | bytes 1474568 | tf_op jit(solution)/shard_map/core/ppermute | solution.py:22
  80.1 3.3 %collective-permute-start.12 = (bf16[4,32,1920]{2,1,0:T(8,128)(2,1)}, bf16[4,32,1920]{2,1,0:T(8,128)(2,1)}, u32[]{:S(2)}, u32[]{:S(2)}) collective-permute-start(bf16[4,32,1920]{2,1,0:T(8,128)(2,1)} %get-tuple-element.27.refs_4_), channel_id=1, source_target_pairs={{0,64},{1,65},{2,66},{3,67},{8,72},{9,73},{10,74},{11,75},{16,80},... | collective-permute-start | bytes 1474568 | tf_op jit(solution)/shard_map/dup_z2/ppermute | solution.py:22
  86.4 3.7 %shard_map.84.refs_2_ = bf16[2,4,2,8,32,1920]{5,4,3,2,1,0:T(8,128)(2,1)} custom-call(s32[18]{0:T(128)S(1)} %stack.40.index_ref, bf16[8,32,1920]{2,1,0:T(8,128)(2,1)} %collective-permute-done.refs_0_, bf16[8,32,1920]{2,1,0:T(8,128)(2,1)} %collective-permute-done.14.refs_1_, ...), custom_call_target="tpu_custom_call", output_to_operand_aliasing={{}: (7, {})} | custom-call | tf_op jit(solution)/shard_map/pallas_call | solution.py:147
  90.2 2.2 %shard_map.85.refs_6_ = bf16[2,4,2,8,32,1920]{5,4,3,2,1,0:T(8,128)(2,1)} custom-call(s32[6]{0:T(128)S(1)} %stack.39.index_ref, bf16[4,32,1920]{2,1,0:T(8,128)(2,1)} %get-tuple-element.26.refs_0_, bf16[4,32,1920]{2,1,0:T(8,128)(2,1)} %collective-permute-done.13.refs_1_, bf16[2,4,2,8,32,1920]{5,4,3,2,1,0:T(8,128)(2,1)} %shard_map.84.refs_2_), custom_call_target="tpu_custom_call", output_to_operand_aliasing={{}: (3, {})} | custom-call | tf_op jit(solution)/shard_map/pallas_call | solution.py:147
  92.4 1.3 %collective-permute-done.11.refs_2_ = bf16[4,32,1920]{2,1,0:T(8,128)(2,1)S(1)} collective-permute-done((bf16[4,32,1920]{2,1,0:T(8,128)(2,1)}, bf16[4,32,1920]{2,1,0:T(8,128)(2,1)S(1)}, u32[]{:S(2)}, u32[]{:S(2)}) %collective-permute-start.11) | collective-permute-done | bytes 491552 | tf_op jit(solution)/shard_map/dup_x2/ppermute | solution.py:22
  93.7 1.4 %collective-permute-done.12.refs_3_ = bf16[4,32,1920]{2,1,0:T(8,128)(2,1)} collective-permute-done((bf16[4,32,1920]{2,1,0:T(8,128)(2,1)}, bf16[4,32,1920]{2,1,0:T(8,128)(2,1)}, u32[]{:S(2)}, u32[]{:S(2)}) %collective-permute-start.12) | collective-permute-done | bytes 491552 | tf_op jit(solution)/shard_map/dup_z2/ppermute | solution.py:22
  96.6 2.5 %shard_map.87.refs_4_ = bf16[2,4,2,8,32,1920]{5,4,3,2,1,0:T(8,128)(2,1)} custom-call(s32[12]{0:T(128)S(1)} %stack.41.index_ref, bf16[4,32,1920]{2,1,0:T(8,128)(2,1)S(1)} %get-tuple-element.31.refs_0_, bf16[8,32,1920]{2,1,0:T(8,128)(2,1)S(1)} %get-tuple-element.32.refs_1_, ...), custom_call_target="tpu_custom_call", output_to_operand_aliasing={{}: (5, {})} | custom-call | tf_op jit(solution)/shard_map/pallas_call | solution.py:147
  99.1 1.8 %collective-permute-done.21 = f32[64,512]{1,0:T(8,128)S(1)} collective-permute-done((f32[64,512]{1,0:T(8,128)S(1)}, f32[64,512]{1,0:T(8,128)S(1)}, u32[]{:S(2)}, u32[]{:S(2)}) %collective-permute-start.21) | collective-permute-done | bytes 131104 | tf_op jit(solution)/shard_map/sum_z/ppermute | solution.py:238
  101.7 2.8 %shard_map.88 = bf16[2,4,2,8,32,1920]{5,4,3,2,1,0:T(8,128)(2,1)} custom-call(s32[12]{0:T(128)S(1)} %stack.33.index_ref, bf16[4,32,1920]{2,1,0:T(8,128)(2,1)S(1)} %collective-permute-done.17.refs_0_, bf16[8,32,1920]{2,1,0:T(8,128)(2,1)} %collective-permute-done.18.refs_1_, ...), custom_call_target="tpu_custom_call", output_to_operand_aliasing={{}: (5, {})} | custom-call | tf_op jit(solution)/shard_map/pallas_call | solution.py:147
  (57 shorter events, 12.4 us)
Async XLA Ops:
  0.6 1.5 %copy-start = (f32[32,15360]{1,0:T(8,128)S(1)}, f32[32,15360]{1,0:T(8,128)}, u32[]{:S(2)}) copy-start(f32[32,15360]{1,0:T(8,128)} %in_ref.1) | copy-start | bytes 5898244
  3.2 21.5 %all-to-all-start = ((bf16[8,32,1920]{2,1,0:T(8,128)(2,1)}), bf16[8,32,1920]{2,1,0:T(8,128)(2,1)S(1)}, u32[]{:S(2)}, u32[]{:S(2)}) async-start(bf16[8,32,1920]{2,1,0:T(8,128)(2,1)} %shard_map.77.after_ref), calls=%async_computation | async-start | bytes 1966080 | tf_op jit(solution)/shard_map/over_t/all_to_all | solution.py:193
  9.6 0.8 copy-start.5
  10.4 0.8 copy-start.6
  11.2 0.7 copy-start.7
  24.7 10.5 %collective-permute-start.5 = (bf16[8,32,1920]{2,1,0:T(8,128)(2,1)S(1)}, bf16[8,32,1920]{2,1,0:T(8,128)(2,1)}, u32[]{:S(2)}, u32[]{:S(2)}) collective-permute-start(bf16[8,32,1920]{2,1,0:T(8,128)(2,1)S(1)} %get-tuple-element.20.refs_0_), channel_id=1, source_target_pairs={{0,8},{1,9},{2,10},{3,11},{8,0},{9,1},{10,2},{11,3},{16,24},{17,25... | collective-permute-start | bytes 2949128 | tf_op jit(solution)/shard_map/core/ppermute | solution.py:22
  25.5 24.7 %collective-permute-start.3 = (bf16[8,32,1920]{2,1,0:T(8,128)(2,1)S(1)}, bf16[8,32,1920]{2,1,0:T(8,128)(2,1)S(1)}, u32[]{:S(2)}, u32[]{:S(2)}) collective-permute-start(bf16[8,32,1920]{2,1,0:T(8,128)(2,1)S(1)} %get-tuple-element.20.refs_0_), channel_id=1, source_target_pairs={{0,16},{1,17},{2,18},{3,19},{8,24},{9,25},{10,26},{11,27},{16,32},... | collective-permute-start | bytes 2949128 | tf_op jit(solution)/shard_map/own_x/ppermute | solution.py:22
  26.8 23.5 %collective-permute-start.4 = (bf16[8,32,1920]{2,1,0:T(8,128)(2,1)S(1)}, bf16[8,32,1920]{2,1,0:T(8,128)(2,1)}, u32[]{:S(2)}, u32[]{:S(2)}) collective-permute-start(bf16[8,32,1920]{2,1,0:T(8,128)(2,1)S(1)} %get-tuple-element.20.refs_0_), channel_id=1, source_target_pairs={{0,48},{1,49},{2,50},{3,51},{8,56},{9,57},{10,58},{11,59},{16,0},{... | collective-permute-start | bytes 2949128 | tf_op jit(solution)/shard_map/own_x/ppermute | solution.py:22
  28.2 18.2 %all-to-all-start.1 = ((f32[4,2,64,512]{3,2,1,0:T(8,128)}), f32[4,2,64,512]{3,2,1,0:T(8,128)S(1)}, u32[]{:S(2)}, u32[]{:S(2)}) async-start(f32[4,2,64,512]{3,2,1,0:T(8,128)} %get-tuple-element.21), calls=%async_computation.1 | async-start | bytes 2097152 | tf_op jit(solution)/shard_map/sum_y/all_to_all | solution.py:203
  31.9 25.0 %collective-permute-start = (bf16[8,32,1920]{2,1,0:T(8,128)(2,1)S(1)}, bf16[8,32,1920]{2,1,0:T(8,128)(2,1)}, u32[]{:S(2)}, u32[]{:S(2)}) collective-permute-start(bf16[8,32,1920]{2,1,0:T(8,128)(2,1)S(1)} %get-tuple-element.20.refs_0_), channel_id=1, source_target_pairs={{0,64},{1,65},{2,66},{3,67},{8,72},{9,73},{10,74},{11,75},{16,80},... | collective-permute-start | bytes 2949128 | tf_op jit(solution)/shard_map/over_z/ppermute | solution.py:22
  50.3 9.5 %collective-permute-start.10 = (bf16[8,32,1920]{2,1,0:T(8,128)(2,1)}, bf16[8,32,1920]{2,1,0:T(8,128)(2,1)S(1)}, u32[]{:S(2)}, u32[]{:S(2)}) collective-permute-start(bf16[8,32,1920]{2,1,0:T(8,128)(2,1)} %get-tuple-element.23.refs_2_), channel_id=1, source_target_pairs={{0,8},{1,9},{2,10},{3,11},{8,0},{9,1},{10,2},{11,3},{16,24},{17,25... | collective-permute-start | bytes 2949128 | tf_op jit(solution)/shard_map/core/ppermute | solution.py:22
  51.0 12.4 %collective-permute-start.9 = (bf16[8,32,1920]{2,1,0:T(8,128)(2,1)S(1)}, bf16[8,32,1920]{2,1,0:T(8,128)(2,1)}, u32[]{:S(2)}, u32[]{:S(2)}) collective-permute-start(bf16[8,32,1920]{2,1,0:T(8,128)(2,1)S(1)} %get-tuple-element.22.refs_0_), channel_id=1, source_target_pairs={{0,8},{1,9},{2,10},{3,11},{8,0},{9,1},{10,2},{11,3},{16,24},{17,25... | collective-permute-start | bytes 2949128 | tf_op jit(solution)/shard_map/core/ppermute | solution.py:22
  53.7 14.4 %collective-permute-start.6 = (bf16[4,32,1920]{2,1,0:T(8,128)(2,1)}, bf16[4,32,1920]{2,1,0:T(8,128)(2,1)S(1)}, u32[]{:S(2)}, u32[]{:S(2)}) collective-permute-start(bf16[4,32,1920]{2,1,0:T(8,128)(2,1)} %slice.10), channel_id=1, source_target_pairs={{0,16},{1,17},{2,18},{3,19},{8,24},{9,25},{10,26},{11,27},{16,32},... | collective-permute-start | bytes 1474568 | tf_op jit(solution)/shard_map/own_x2/ppermute | solution.py:22
  55.0 16.0 %collective-permute-start.7 = (bf16[4,32,1920]{2,1,0:T(8,128)(2,1)}, bf16[4,32,1920]{2,1,0:T(8,128)(2,1)}, u32[]{:S(2)}, u32[]{:S(2)}) collective-permute-start(bf16[4,32,1920]{2,1,0:T(8,128)(2,1)} %slice.11), channel_id=1, source_target_pairs={{0,48},{1,49},{2,50},{3,51},{8,56},{9,57},{10,58},{11,59},{16,0},{... | collective-permute-start | bytes 1474568 | tf_op jit(solution)/shard_map/own_x2/ppermute | solution.py:22
  56.9 14.0 %collective-permute-start.8 = (bf16[4,32,1920]{2,1,0:T(8,128)(2,1)}, bf16[4,32,1920]{2,1,0:T(8,128)(2,1)}, u32[]{:S(2)}, u32[]{:S(2)}) collective-permute-start(bf16[4,32,1920]{2,1,0:T(8,128)(2,1)} %slice.10), channel_id=1, source_target_pairs={{0,64},{1,65},{2,66},{3,67},{8,72},{9,73},{10,74},{11,75},{16,80},... | collective-permute-start | bytes 1474568 | tf_op jit(solution)/shard_map/dup_z/ppermute | solution.py:22
  59.7 1.0 copy-start.1
  60.7 18.6 %collective-permute-start.14 = (bf16[8,32,1920]{2,1,0:T(8,128)(2,1)}, bf16[8,32,1920]{2,1,0:T(8,128)(2,1)}, u32[]{:S(2)}, u32[]{:S(2)}) collective-permute-start(bf16[8,32,1920]{2,1,0:T(8,128)(2,1)} %collective-permute-done.refs_0_), channel_id=1, source_target_pairs={{0,8},{1,9},{2,10},{3,11},{8,0},{9,1},{10,2},{11,3},{16,24},{17,25... | collective-permute-start | bytes 2949128 | tf_op jit(solution)/shard_map/core/ppermute | solution.py:22
  63.4 14.6 %collective-permute-start.1 = (bf16[4,32,1920]{2,1,0:T(8,128)(2,1)S(1)}, bf16[4,32,1920]{2,1,0:T(8,128)(2,1)S(1)}, u32[]{:S(2)}, u32[]{:S(2)}) collective-permute-start(bf16[4,32,1920]{2,1,0:T(8,128)(2,1)S(1)} %slice.12), channel_id=1, source_target_pairs={{0,16},{1,17},{2,18},{3,19},{8,24},{9,25},{10,26},{11,27},{16,32},... | collective-permute-start | bytes 1474568 | tf_op jit(solution)/shard_map/dup_x/ppermute | solution.py:22
  63.5 1.2 %copy-start.2 = (bf16[8,32,1920]{2,1,0:T(8,128)(2,1)S(1)}, bf16[8,32,1920]{2,1,0:T(8,128)(2,1)}, u32[]{:S(2)}) copy-start(bf16[8,32,1920]{2,1,0:T(8,128)(2,1)} %copy-done.1) | copy-start | bytes 2949124
  68.2 24.2 %collective-permute-start.2 = (bf16[8,32,1920]{2,1,0:T(8,128)(2,1)}, bf16[8,32,1920]{2,1,0:T(8,128)(2,1)S(1)}, u32[]{:S(2)}, u32[]{:S(2)}) collective-permute-start(bf16[8,32,1920]{2,1,0:T(8,128)(2,1)} %collective-permute-done.refs_0_), channel_id=1, source_target_pairs={{0,48},{1,49},{2,50},{3,51},{8,56},{9,57},{10,58},{11,59},{16,0},{... | collective-permute-start | bytes 2949128 | tf_op jit(solution)/shard_map/dup_x/ppermute | solution.py:22
  70.9 8.4 %collective-permute-start.15 = (bf16[4,32,1920]{2,1,0:T(8,128)(2,1)S(1)}, bf16[4,32,1920]{2,1,0:T(8,128)(2,1)S(1)}, u32[]{:S(2)}, u32[]{:S(2)}) collective-permute-start(bf16[4,32,1920]{2,1,0:T(8,128)(2,1)S(1)} %get-tuple-element.29.refs_2_), channel_id=1, source_target_pairs={{0,8},{1,9},{2,10},{3,11},{8,0},{9,1},{10,2},{11,3},{16,24},{17,25... | collective-permute-start | bytes 1474568 | tf_op jit(solution)/shard_map/core/ppermute | solution.py:22
  72.4 13.0 %collective-permute-start.16 = (bf16[4,32,1920]{2,1,0:T(8,128)(2,1)}, bf16[4,32,1920]{2,1,0:T(8,128)(2,1)}, u32[]{:S(2)}, u32[]{:S(2)}) collective-permute-start(bf16[4,32,1920]{2,1,0:T(8,128)(2,1)} %get-tuple-element.27.refs_4_), channel_id=1, source_target_pairs={{0,8},{1,9},{2,10},{3,11},{8,0},{9,1},{10,2},{11,3},{16,24},{17,25... | collective-permute-start | bytes 1474568 | tf_op jit(solution)/shard_map/core/ppermute | solution.py:22
  78.0 12.2 %collective-permute-start.13 = (bf16[4,32,1920]{2,1,0:T(8,128)(2,1)}, bf16[4,32,1920]{2,1,0:T(8,128)(2,1)}, u32[]{:S(2)}, u32[]{:S(2)}) collective-permute-start(bf16[4,32,1920]{2,1,0:T(8,128)(2,1)} %get-tuple-element.26.refs_0_), channel_id=1, source_target_pairs={{0,8},{1,9},{2,10},{3,11},{8,0},{9,1},{10,2},{11,3},{16,24},{17,25... | collective-permute-start | bytes 1474568 | tf_op jit(solution)/shard_map/core/ppermute | solution.py:22
  79.3 14.4 %collective-permute-start.11 = (bf16[4,32,1920]{2,1,0:T(8,128)(2,1)}, bf16[4,32,1920]{2,1,0:T(8,128)(2,1)S(1)}, u32[]{:S(2)}, u32[]{:S(2)}) collective-permute-start(bf16[4,32,1920]{2,1,0:T(8,128)(2,1)} %get-tuple-element.26.refs_0_), channel_id=1, source_target_pairs={{0,16},{1,17},{2,18},{3,19},{8,24},{9,25},{10,26},{11,27},{16,32},... | collective-permute-start | bytes 1474568 | tf_op jit(solution)/shard_map/dup_x2/ppermute | solution.py:22
  79.3 0.8 copy-start.3
  80.1 15.0 %collective-permute-start.12 = (bf16[4,32,1920]{2,1,0:T(8,128)(2,1)}, bf16[4,32,1920]{2,1,0:T(8,128)(2,1)}, u32[]{:S(2)}, u32[]{:S(2)}) collective-permute-start(bf16[4,32,1920]{2,1,0:T(8,128)(2,1)} %get-tuple-element.27.refs_4_), channel_id=1, source_target_pairs={{0,64},{1,65},{2,66},{3,67},{8,72},{9,73},{10,74},{11,75},{16,80},... | collective-permute-start | bytes 1474568 | tf_op jit(solution)/shard_map/dup_z2/ppermute | solution.py:22
  85.4 1.0 copy-start.4
  95.1 6.5 %collective-permute-start.18 = (bf16[8,32,1920]{2,1,0:T(8,128)(2,1)S(1)}, bf16[8,32,1920]{2,1,0:T(8,128)(2,1)}, u32[]{:S(2)}, u32[]{:S(2)}) collective-permute-start(bf16[8,32,1920]{2,1,0:T(8,128)(2,1)S(1)} %get-tuple-element.32.refs_1_), channel_id=1, source_target_pairs={{0,8},{1,9},{2,10},{3,11},{8,0},{9,1},{10,2},{11,3},{16,24},{17,25... | collective-permute-start | bytes 2949128 | tf_op jit(solution)/shard_map/core/ppermute | solution.py:22
  95.9 5.7 %collective-permute-start.17 = (bf16[4,32,1920]{2,1,0:T(8,128)(2,1)S(1)}, bf16[4,32,1920]{2,1,0:T(8,128)(2,1)S(1)}, u32[]{:S(2)}, u32[]{:S(2)}) collective-permute-start(bf16[4,32,1920]{2,1,0:T(8,128)(2,1)S(1)} %get-tuple-element.31.refs_0_), channel_id=1, source_target_pairs={{0,8},{1,9},{2,10},{3,11},{8,0},{9,1},{10,2},{11,3},{16,24},{17,25... | collective-permute-start | bytes 1474568 | tf_op jit(solution)/shard_map/core/ppermute | solution.py:22
  95.9 5.7 %collective-permute-start.19 = (bf16[4,32,1920]{2,1,0:T(8,128)(2,1)S(1)}, bf16[4,32,1920]{2,1,0:T(8,128)(2,1)S(1)}, u32[]{:S(2)}, u32[]{:S(2)}) collective-permute-start(bf16[4,32,1920]{2,1,0:T(8,128)(2,1)S(1)} %get-tuple-element.33.refs_2_), channel_id=1, source_target_pairs={{0,8},{1,9},{2,10},{3,11},{8,0},{9,1},{10,2},{11,3},{16,24},{17,25... | collective-permute-start | bytes 1474568 | tf_op jit(solution)/shard_map/core/ppermute | solution.py:22
  96.4 5.2 %collective-permute-start.20 = (bf16[4,32,1920]{2,1,0:T(8,128)(2,1)}, bf16[4,32,1920]{2,1,0:T(8,128)(2,1)}, u32[]{:S(2)}, u32[]{:S(2)}) collective-permute-start(bf16[4,32,1920]{2,1,0:T(8,128)(2,1)} %get-tuple-element.34.refs_3_), channel_id=1, source_target_pairs={{0,8},{1,9},{2,10},{3,11},{8,0},{9,1},{10,2},{11,3},{16,24},{17,25... | collective-permute-start | bytes 1474568 | tf_op jit(solution)/shard_map/core/ppermute | solution.py:22
  96.4 4.6 %collective-permute-start.21 = (f32[64,512]{1,0:T(8,128)S(1)}, f32[64,512]{1,0:T(8,128)S(1)}, u32[]{:S(2)}, u32[]{:S(2)}) collective-permute-start(f32[64,512]{1,0:T(8,128)S(1)} %get-tuple-element.37), channel_id=1, source_target_pairs={{0,4},{1,5},{2,6},{3,7},{4,0},{5,1},{6,2},{7,3},{8,12},{9,13},{10,... | collective-permute-start | bytes 393224 | tf_op jit(solution)/shard_map/sum_z/ppermute | solution.py:238

commit v3 on v2

--- a/solution.py
+++ b/solution.py
@@ -123,6 +123,31 @@
     )
 
 
+def halves(left, right):
+    shape = (left.shape[0] // 2,) + left.shape[1:]
+
+    def kernel(left_ref, right_ref, low_ref, high_ref, sem):
+        half = shape[0]
+        copies = [
+            pltpu.make_async_copy(left_ref.at[pl.ds(0, half)], low_ref, sem.at[0]),
+            pltpu.make_async_copy(right_ref.at[pl.ds(half, half)], high_ref, sem.at[1]),
+        ]
+        for copy in copies:
+            copy.start()
+        for copy in copies:
+            copy.wait()
+
+    return pl.pallas_call(
+        kernel,
+        in_specs=[pl.BlockSpec(memory_space=pl.ANY)] * 2,
+        out_specs=[pl.BlockSpec(memory_space=pltpu.VMEM)] * 2,
+        out_shape=[jax.ShapeDtypeStruct(shape, left.dtype)] * 2,
+        scratch_shapes=[pltpu.SemaphoreType.DMA((2,))],
+        compiler_params=pltpu.CompilerParams(vmem_limit_bytes=4 << 20),
+        cost_estimate=pl.CostEstimate(flops=0, bytes_accessed=0, transcendentals=0),
+    )(left, right)
+
+
 def place(out, pieces):
     shape = (2, 4, 2, 8) + pieces[0][0].shape[1:]
     index = jnp.stack([jnp.int32(v) for p in pieces for v in p[2:]])
@@ -207,7 +232,7 @@
     out = place(None, both(own, z_hi, 0))
     own_1, own_3, shares, out = fence(own_1, own_3, shares, out)
 
-    low_1, high_3 = own_1[:4], own_3[4:]
+    low_1, high_3 = halves(own_1, own_3)
     with jax.named_scope("own_x2"):
         low_2, high_2 = send(low_1, dx=1), send(high_3, dx=-1)
     with jax.named_scope("dup_z"):
@@ -224,19 +249,20 @@
         dup_high_2 = send(high_2, dz=2)
     total = jnp.sum(shares, axis=0)
     kept, given = pick(total, z_lo), pick(total, 1 - z_lo)
+    out = place(out, both(dup_low_1, 1 - z_hi, 1))
     out = place(out, both(dup, 1 - z_hi, 0) + both(low_2, z_hi, 2) + both(high_2, z_hi, 2, 4))
-    out = place(out, both(dup_low_1, 1 - z_hi, 1))
     dup_high_1, dup_3, dup_low_2, dup_high_2, kept, given, out = fence(
         dup_high_1, dup_3, dup_low_2, dup_high_2, kept, given, out
     )
 
+    with jax.named_scope("sum_z"):
+        given = lax.ppermute(given, AXES, [(i, i ^ 4) for i in range(128)])
     pairs = [both(dup_high_1, 1 - z_hi, 1, 4), both(dup_3, 1 - z_hi, 3)]
     pairs += [both(dup_low_2, 1 - z_hi, 2), both(dup_high_2, 1 - z_hi, 2, 4)]
     out = place(out, [mine for mine, _ in pairs])
     out = place(out, [theirs for _, theirs in pairs])
-    with jax.named_scope("sum_z"):
-        attn = kept + lax.ppermute(given, AXES, [(i, i ^ 4) for i in range(128)])
-        attn = attn.astype(jnp.bfloat16)
+    out, kept, given = fence(out, kept, given)
+    attn = (kept + given).astype(jnp.bfloat16)
     return (out.reshape(-1, width), attn.reshape(r, s, -1))
 
 

time: 105 us -> 104 us (level)
  local copies, waits for them, and re-layouts: 13 us -> 10.3 us
  Pallas kernels: 27 us -> 28.7 us
    slice x2 -> x0, local copies, waits for them, and re-layouts: 2.7 us -> none  [local(): low_1, high_3 = (own_1[:4], own_3[4:])]
    ppermute x21, waiting for transfers between devices: 12.7 us -> 14.9 us  [send(): return lax.ppermute(value, AXES, pairs)]
    ppermute x1, waiting for transfers between devices: 1.85 us -> 0.01 us  [local(): given = lax.ppermute(given, AXES, [(i, i ^ 4) for i in range(128)])]
    pallas_call x0 -> x1, Pallas kernels: none -> 1.59 us  [halves(): pl.pallas_call(kernel, in_specs=[pl.BlockSpec(memory_space=pl.ANY)] * 2,...]
  transfers between devices with their start and end apart: 24 -> 24, of which waited for: 8 -> 11; matrix products, arithmetic and copies ran while one was open for 6% -> 3% of each run, Pallas kernels for 22% -> 27%
where the time goes in v3:
time: 104 us; the launch traced here: 103 us
  starting transfers between devices  34.4 us (33%)
  Pallas kernels  28.7 us (28%)
  waiting for transfers between devices  27.5 us (26%)
  local copies, waits for them, and re-layouts  10.3 us (10%)
  other arithmetic  1.45 us (1%)
    ppermute x21, starting transfers between devices, send(): return lax.ppermute(value, AXES, pairs)  24.6 us
    pallas_call x6, Pallas kernels, place(): pl.pallas_call(kernel, in_specs=specs, out_specs=pl.BlockSpec(memory_spac...  17.3 us
    ppermute x21, waiting for transfers between devices, send(): return lax.ppermute(value, AXES, pairs)  14.9 us
    pallas_call x1, Pallas kernels, attend(): pl.pallas_call(kernel, in_specs=[pl.BlockSpec(memory_space=pltpu.SMEM), v...  8.77 us
    all_to_all x1, waiting for transfers between devices, local(): lax.all_to_all(shares, 'tp', split_axis=0, concat_axis=0, tiled=True, axi...  8.42 us
    unnamed x16, local copies, waits for them, and re-layouts  7.71 us
    all_to_all x1, starting transfers between devices, local(): own = lax.all_to_all(blocks, 'tp', split_axis=0, concat_axis=0, tiled=True)  6.37 us
    all_to_all x1, waiting for transfers between devices, local(): own = lax.all_to_all(blocks, 'tp', split_axis=0, concat_axis=0, tiled=True)  4.19 us
  transfers between devices with their start and end apart: 24, of which 11 were waited for; matrix products, arithmetic and copies ran while one was open for 3% of the time, Pallas kernels for 27%

profile of v3, /device:TPU:1, one launch (start us, length us, event | category | flops | bytes accessed | tf_op | source)
XLA Modules:
  0.0 103.3 jit_solution(7950349440622509640)
XLA Ops:
  0.6 1.5 %copy-done = f32[32,15360]{1,0:T(8,128)S(1)} copy-done((f32[32,15360]{1,0:T(8,128)S(1)}, f32[32,15360]{1,0:T(8,128)}, u32[]{:S(2)}) %copy-start) | copy-done | bytes 1966104
  2.2 1.0 %shard_map.77.after_ref = bf16[8,32,1920]{2,1,0:T(8,128)(2,1)} custom-call(f32[32,15360]{1,0:T(8,128)S(1)} %copy-done), custom_call_target="tpu_custom_call" | custom-call | tf_op jit(solution)/shard_map/pallas_call | solution.py:33
  3.2 6.4 %all-to-all-start = ((bf16[8,32,1920]{2,1,0:T(8,128)(2,1)}), bf16[8,32,1920]{2,1,0:T(8,128)(2,1)}, u32[]{:S(2)}, u32[]{:S(2)}) async-start(bf16[8,32,1920]{2,1,0:T(8,128)(2,1)} %shard_map.77.after_ref), calls=%async_computation | async-start | bytes 1966080 | tf_op jit(solution)/shard_map/over_t/all_to_all | solution.py:218
  11.8 8.8 %shard_map.78.refs_1_ = f32[4,2,64,512]{3,2,1,0:T(8,128)} custom-call(s32[8]{0:T(128)S(1)} %copy-done.7, bf16[8,8,512]{2,1,0:T(8,128)(2,1)S(1)} %copy-done.5, bf16[8,8,2,128]{3,2,1,0:T(2,128)(2,1)S(1)} %copy-done.6, bf16[8,2,1,1024,128]{4,3,2,1,0:T(8,128)(2,1)} %cache_hbm.1, bf16[512,4096]{1,0:T(8,128)(2,1)} %weight_hbm.1, ...), custom_call_target="tpu_custom_call" | custom-call | flops 1 | bytes 1 | tf_op jit(solution)/shard_map/pallas_call | solution.py:99
  20.6 4.2 %all-to-all-done.refs_0_ = bf16[8,32,1920]{2,1,0:T(8,128)(2,1)} async-done(((bf16[8,32,1920]{2,1,0:T(8,128)(2,1)}), bf16[8,32,1920]{2,1,0:T(8,128)(2,1)}, u32[]{:S(2)}, u32[]{:S(2)}) %all-to-all-start) | async-done | bytes 983072 | tf_op jit(solution)/shard_map/over_t/all_to_all | solution.py:218
  25.7 1.2 %collective-permute-start.3 = (bf16[8,32,1920]{2,1,0:T(8,128)(2,1)}, bf16[8,32,1920]{2,1,0:T(8,128)(2,1)S(1)}, u32[]{:S(2)}, u32[]{:S(2)}) collective-permute-start(bf16[8,32,1920]{2,1,0:T(8,128)(2,1)} %get-tuple-element.25.refs_0_), channel_id=1, source_target_pairs={{0,16},{1,17},{2,18},{3,19},{8,24},{9,25},{10,26},{11,27},{16,32},... | collective-permute-start | bytes 2949128 | tf_op jit(solution)/shard_map/own_x/ppermute | solution.py:22
  26.9 1.5 %collective-permute-start.4 = (bf16[8,32,1920]{2,1,0:T(8,128)(2,1)}, bf16[8,32,1920]{2,1,0:T(8,128)(2,1)S(1)}, u32[]{:S(2)}, u32[]{:S(2)}) collective-permute-start(bf16[8,32,1920]{2,1,0:T(8,128)(2,1)} %get-tuple-element.25.refs_0_), channel_id=1, source_target_pairs={{0,48},{1,49},{2,50},{3,51},{8,56},{9,57},{10,58},{11,59},{16,0},{... | collective-permute-start | bytes 2949128 | tf_op jit(solution)/shard_map/own_x/ppermute | solution.py:22
  28.3 3.5 %all-to-all-start.1 = ((f32[4,2,64,512]{3,2,1,0:T(8,128)}), f32[4,2,64,512]{3,2,1,0:T(8,128)S(1)}, u32[]{:S(2)}, u32[]{:S(2)}) async-start(f32[4,2,64,512]{3,2,1,0:T(8,128)} %get-tuple-element.26), calls=%async_computation.1 | async-start | bytes 2097152 | tf_op jit(solution)/shard_map/sum_y/all_to_all | solution.py:228
  32.0 3.3 %collective-permute-start = (bf16[8,32,1920]{2,1,0:T(8,128)(2,1)}, bf16[8,32,1920]{2,1,0:T(8,128)(2,1)}, u32[]{:S(2)}, u32[]{:S(2)}) collective-permute-start(bf16[8,32,1920]{2,1,0:T(8,128)(2,1)} %get-tuple-element.25.refs_0_), channel_id=1, source_target_pairs={{0,64},{1,65},{2,66},{3,67},{8,72},{9,73},{10,74},{11,75},{16,80},... | collective-permute-start | bytes 2949128 | tf_op jit(solution)/shard_map/over_z/ppermute | solution.py:22
  35.3 2.8 %shard_map.80.refs_3_ = bf16[2,4,2,8,32,1920]{5,4,3,2,1,0:T(8,128)(2,1)} custom-call(s32[6]{0:T(128)S(1)} %stack.37.index_ref, bf16[8,32,1920]{2,1,0:T(8,128)(2,1)} %get-tuple-element.25.refs_0_, bf16[8,32,1920]{2,1,0:T(8,128)(2,1)} %collective-permute-done.5.refs_1_), custom_call_target="tpu_custom_call" | custom-call | tf_op jit(solution)/shard_map/pallas_call | solution.py:172
  38.1 8.4 %all-to-all-done.1.refs_2_ = f32[4,2,64,512]{3,2,1,0:T(8,128)S(1)} async-done(((f32[4,2,64,512]{3,2,1,0:T(8,128)}), f32[4,2,64,512]{3,2,1,0:T(8,128)S(1)}, u32[]{:S(2)}, u32[]{:S(2)}) %all-to-all-start.1) | async-done | bytes 1048608 | tf_op jit(solution)/shard_map/sum_y/all_to_all | solution.py:228
  46.6 4.0 %collective-permute-done.3.refs_0_ = bf16[8,32,1920]{2,1,0:T(8,128)(2,1)S(1)} collective-permute-done((bf16[8,32,1920]{2,1,0:T(8,128)(2,1)}, bf16[8,32,1920]{2,1,0:T(8,128)(2,1)S(1)}, u32[]{:S(2)}, u32[]{:S(2)}) %collective-permute-start.3) | collective-permute-done | bytes 983072 | tf_op jit(solution)/shard_map/own_x/ppermute | solution.py:22
  51.3 1.6 %shard_map.82 = (bf16[4,32,1920]{2,1,0:T(8,128)(2,1)}, bf16[4,32,1920]{2,1,0:T(8,128)(2,1)}) custom-call(bf16[8,32,1920]{2,1,0:T(8,128)(2,1)S(1)} %get-tuple-element.27.left_ref.refs_0_, bf16[8,32,1920]{2,1,0:T(8,128)(2,1)S(1)} %get-tuple-element.28.right_ref.refs_2_), custom_call_target="tpu_custom_call" | custom-call | tf_op jit(solution)/shard_map/pallas_call | solution.py:140
  52.9 1.2 %collective-permute-start.6 = (bf16[4,32,1920]{2,1,0:T(8,128)(2,1)}, bf16[4,32,1920]{2,1,0:T(8,128)(2,1)}, u32[]{:S(2)}, u32[]{:S(2)}) collective-permute-start(bf16[4,32,1920]{2,1,0:T(8,128)(2,1)} %get-tuple-element.29), channel_id=1, source_target_pairs={{0,16},{1,17},{2,18},{3,19},{8,24},{9,25},{10,26},{11,27},{16,32},... | collective-permute-start | bytes 1474568 | tf_op jit(solution)/shard_map/own_x2/ppermute | solution.py:22
  54.1 1.5 %collective-permute-start.7 = (bf16[4,32,1920]{2,1,0:T(8,128)(2,1)}, bf16[4,32,1920]{2,1,0:T(8,128)(2,1)}, u32[]{:S(2)}, u32[]{:S(2)}) collective-permute-start(bf16[4,32,1920]{2,1,0:T(8,128)(2,1)} %get-tuple-element.30), channel_id=1, source_target_pairs={{0,48},{1,49},{2,50},{3,51},{8,56},{9,57},{10,58},{11,59},{16,0},{... | collective-permute-start | bytes 1474568 | tf_op jit(solution)/shard_map/own_x2/ppermute | solution.py:22
  55.7 1.6 %collective-permute-done.refs_0_ = bf16[8,32,1920]{2,1,0:T(8,128)(2,1)} collective-permute-done((bf16[8,32,1920]{2,1,0:T(8,128)(2,1)}, bf16[8,32,1920]{2,1,0:T(8,128)(2,1)}, u32[]{:S(2)}, u32[]{:S(2)}) %collective-permute-start) | collective-permute-done | bytes 983072 | tf_op jit(solution)/shard_map/over_z/ppermute | solution.py:22
  57.2 2.6 %collective-permute-start.8 = (bf16[4,32,1920]{2,1,0:T(8,128)(2,1)}, bf16[4,32,1920]{2,1,0:T(8,128)(2,1)}, u32[]{:S(2)}, u32[]{:S(2)}) collective-permute-start(bf16[4,32,1920]{2,1,0:T(8,128)(2,1)} %get-tuple-element.29), channel_id=1, source_target_pairs={{0,64},{1,65},{2,66},{3,67},{8,72},{9,73},{10,74},{11,75},{16,80},... | collective-permute-start | bytes 1474568 | tf_op jit(solution)/shard_map/dup_z/ppermute | solution.py:22
  60.8 1.7 %collective-permute-start.13 = (bf16[8,32,1920]{2,1,0:T(8,128)(2,1)}, bf16[8,32,1920]{2,1,0:T(8,128)(2,1)}, u32[]{:S(2)}, u32[]{:S(2)}) collective-permute-start(bf16[8,32,1920]{2,1,0:T(8,128)(2,1)} %collective-permute-done.refs_0_), channel_id=1, source_target_pairs={{0,8},{1,9},{2,10},{3,11},{8,0},{9,1},{10,2},{11,3},{16,24},{17,25... | collective-permute-start | bytes 2949128 | tf_op jit(solution)/shard_map/core/ppermute | solution.py:22
  62.6 1.1 %slice.4 = bf16[4,32,1920]{2,1,0:T(8,128)(2,1)S(1)} slice(bf16[8,32,1920]{2,1,0:T(8,128)(2,1)} %collective-permute-done.refs_0_), slice={[4:8], [0:32], [0:1920]} | slice | bytes 983040 | tf_op jit(solution)/shard_map/dup_x/slice | solution.py:241
  63.8 1.2 %copy-done.2 = bf16[8,32,1920]{2,1,0:T(8,128)(2,1)S(1)} copy-done((bf16[8,32,1920]{2,1,0:T(8,128)(2,1)S(1)}, bf16[8,32,1920]{2,1,0:T(8,128)(2,1)}, u32[]{:S(2)}) %copy-start.2) | copy-done | bytes 983064
  65.0 3.2 %shard_map.83.refs_4_ = bf16[2,4,2,8,32,1920]{5,4,3,2,1,0:T(8,128)(2,1)} custom-call(s32[12]{0:T(128)S(1)} %stack.38.index_ref, bf16[8,32,1920]{2,1,0:T(8,128)(2,1)S(1)} %get-tuple-element.27.left_ref.refs_0_, bf16[8,32,1920]{2,1,0:T(8,128)(2,1)} %collective-permute-done.9.refs_1_, ...), custom_call_target="tpu_custom_call", output_to_operand_aliasing={{}: (5, {})} | custom-call | tf_op jit(solution)/shard_map/pallas_call | solution.py:172
  68.2 2.7 %collective-permute-start.2 = (bf16[8,32,1920]{2,1,0:T(8,128)(2,1)}, bf16[8,32,1920]{2,1,0:T(8,128)(2,1)S(1)}, u32[]{:S(2)}, u32[]{:S(2)}) collective-permute-start(bf16[8,32,1920]{2,1,0:T(8,128)(2,1)} %collective-permute-done.refs_0_), channel_id=1, source_target_pairs={{0,48},{1,49},{2,50},{3,51},{8,56},{9,57},{10,58},{11,59},{16,0},{... | collective-permute-start | bytes 2949128 | tf_op jit(solution)/shard_map/dup_x/ppermute | solution.py:22
  70.9 1.8 %collective-permute-start.16 = (bf16[4,32,1920]{2,1,0:T(8,128)(2,1)}, bf16[4,32,1920]{2,1,0:T(8,128)(2,1)S(1)}, u32[]{:S(2)}, u32[]{:S(2)}) collective-permute-start(bf16[4,32,1920]{2,1,0:T(8,128)(2,1)} %get-tuple-element.33.refs_0_), channel_id=1, source_target_pairs={{0,8},{1,9},{2,10},{3,11},{8,0},{9,1},{10,2},{11,3},{16,24},{17,25... | collective-permute-start | bytes 1474568 | tf_op jit(solution)/shard_map/core/ppermute | solution.py:22
  72.7 5.1 %collective-permute-done.1.refs_0_ = bf16[4,32,1920]{2,1,0:T(8,128)(2,1)S(1)} collective-permute-done((bf16[4,32,1920]{2,1,0:T(8,128)(2,1)S(1)}, bf16[4,32,1920]{2,1,0:T(8,128)(2,1)S(1)}, u32[]{:S(2)}, u32[]{:S(2)}) %collective-permute-start.1) | collective-permute-done | bytes 491552 | tf_op jit(solution)/shard_map/dup_x/ppermute | solution.py:22
  79.4 3.3 %collective-permute-start.12 = (bf16[4,32,1920]{2,1,0:T(8,128)(2,1)}, bf16[4,32,1920]{2,1,0:T(8,128)(2,1)}, u32[]{:S(2)}, u32[]{:S(2)}) collective-permute-start(bf16[4,32,1920]{2,1,0:T(8,128)(2,1)} %get-tuple-element.34.refs_4_), channel_id=1, source_target_pairs={{0,64},{1,65},{2,66},{3,67},{8,72},{9,73},{10,74},{11,75},{16,80},... | collective-permute-start | bytes 1474568 | tf_op jit(solution)/shard_map/dup_z2/ppermute | solution.py:22
  83.7 1.0 dynamic-slice_bitcast_fusion
  84.7 1.0 copy-done.4
  85.7 2.0 %shard_map.85.refs_6_ = bf16[2,4,2,8,32,1920]{5,4,3,2,1,0:T(8,128)(2,1)} custom-call(s32[6]{0:T(128)S(1)} %stack.40.index_ref, bf16[4,32,1920]{2,1,0:T(8,128)(2,1)} %get-tuple-element.33.refs_0_, bf16[4,32,1920]{2,1,0:T(8,128)(2,1)S(1)} %copy-done.4, bf16[2,4,2,8,32,1920]{5,4,3,2,1,0:T(8,128)(2,1)} %get-tuple-element.37.refs_2_), custom_call_target="tpu_custom_call", output_to_operand_aliasing={{}: (3, {})} | custom-call | tf_op jit(solution)/shard_map/pallas_call | solution.py:172
  87.7 4.0 %shard_map.86.refs_6_ = bf16[2,4,2,8,32,1920]{5,4,3,2,1,0:T(8,128)(2,1)} custom-call(s32[18]{0:T(128)S(1)} %stack.39.index_ref, bf16[8,32,1920]{2,1,0:T(8,128)(2,1)} %collective-permute-done.refs_0_, bf16[8,32,1920]{2,1,0:T(8,128)(2,1)} %collective-permute-done.13.refs_1_, ...), custom_call_target="tpu_custom_call", output_to_operand_aliasing={{}: (7, {})} | custom-call | tf_op jit(solution)/shard_map/pallas_call | solution.py:172
  93.0 1.5 %collective-permute-done.12.refs_3_ = bf16[4,32,1920]{2,1,0:T(8,128)(2,1)} collective-permute-done((bf16[4,32,1920]{2,1,0:T(8,128)(2,1)}, bf16[4,32,1920]{2,1,0:T(8,128)(2,1)}, u32[]{:S(2)}, u32[]{:S(2)}) %collective-permute-start.12) | collective-permute-done | bytes 491552 | tf_op jit(solution)/shard_map/dup_z2/ppermute | solution.py:22
  95.9 2.5 %shard_map.88.refs_4_ = bf16[2,4,2,8,32,1920]{5,4,3,2,1,0:T(8,128)(2,1)} custom-call(s32[12]{0:T(128)S(1)} %stack.41.index_ref, bf16[4,32,1920]{2,1,0:T(8,128)(2,1)S(1)} %get-tuple-element.38.refs_0_, bf16[8,32,1920]{2,1,0:T(8,128)(2,1)S(1)} %get-tuple-element.39.refs_1_, ...), custom_call_target="tpu_custom_call", output_to_operand_aliasing={{}: (5, {})} | custom-call | tf_op jit(solution)/shard_map/pallas_call | solution.py:172
  99.8 2.8 %shard_map.89.refs_0_ = bf16[2,4,2,8,32,1920]{5,4,3,2,1,0:T(8,128)(2,1)} custom-call(s32[12]{0:T(128)S(1)} %stack.33.index_ref, bf16[4,32,1920]{2,1,0:T(8,128)(2,1)} %collective-permute-done.17.refs_0_, bf16[8,32,1920]{2,1,0:T(8,128)(2,1)S(1)} %collective-permute-done.18.refs_1_, ...), custom_call_target="tpu_custom_call", output_to_operand_aliasing={{}: (5, {})} | custom-call | tf_op jit(solution)/shard_map/pallas_call | solution.py:172
  (57 shorter events, 12.3 us)
Async XLA Ops:
  0.6 1.5 %copy-start = (f32[32,15360]{1,0:T(8,128)S(1)}, f32[32,15360]{1,0:T(8,128)}, u32[]{:S(2)}) copy-start(f32[32,15360]{1,0:T(8,128)} %in_ref.1) | copy-start | bytes 5898244
  3.2 21.6 %all-to-all-start = ((bf16[8,32,1920]{2,1,0:T(8,128)(2,1)}), bf16[8,32,1920]{2,1,0:T(8,128)(2,1)}, u32[]{:S(2)}, u32[]{:S(2)}) async-start(bf16[8,32,1920]{2,1,0:T(8,128)(2,1)} %shard_map.77.after_ref), calls=%async_computation | async-start | bytes 1966080 | tf_op jit(solution)/shard_map/over_t/all_to_all | solution.py:218
  9.6 0.8 copy-start.5
  10.4 0.8 copy-start.6
  11.2 0.7 copy-start.7
  24.8 10.5 %collective-permute-start.5 = (bf16[8,32,1920]{2,1,0:T(8,128)(2,1)}, bf16[8,32,1920]{2,1,0:T(8,128)(2,1)}, u32[]{:S(2)}, u32[]{:S(2)}) collective-permute-start(bf16[8,32,1920]{2,1,0:T(8,128)(2,1)} %get-tuple-element.25.refs_0_), channel_id=1, source_target_pairs={{0,8},{1,9},{2,10},{3,11},{8,0},{9,1},{10,2},{11,3},{16,24},{17,25... | collective-permute-start | bytes 2949128 | tf_op jit(solution)/shard_map/core/ppermute | solution.py:22
  25.7 24.9 %collective-permute-start.3 = (bf16[8,32,1920]{2,1,0:T(8,128)(2,1)}, bf16[8,32,1920]{2,1,0:T(8,128)(2,1)S(1)}, u32[]{:S(2)}, u32[]{:S(2)}) collective-permute-start(bf16[8,32,1920]{2,1,0:T(8,128)(2,1)} %get-tuple-element.25.refs_0_), channel_id=1, source_target_pairs={{0,16},{1,17},{2,18},{3,19},{8,24},{9,25},{10,26},{11,27},{16,32},... | collective-permute-start | bytes 2949128 | tf_op jit(solution)/shard_map/own_x/ppermute | solution.py:22
  26.9 23.7 %collective-permute-start.4 = (bf16[8,32,1920]{2,1,0:T(8,128)(2,1)}, bf16[8,32,1920]{2,1,0:T(8,128)(2,1)S(1)}, u32[]{:S(2)}, u32[]{:S(2)}) collective-permute-start(bf16[8,32,1920]{2,1,0:T(8,128)(2,1)} %get-tuple-element.25.refs_0_), channel_id=1, source_target_pairs={{0,48},{1,49},{2,50},{3,51},{8,56},{9,57},{10,58},{11,59},{16,0},{... | collective-permute-start | bytes 2949128 | tf_op jit(solution)/shard_map/own_x/ppermute | solution.py:22
  28.3 18.2 %all-to-all-start.1 = ((f32[4,2,64,512]{3,2,1,0:T(8,128)}), f32[4,2,64,512]{3,2,1,0:T(8,128)S(1)}, u32[]{:S(2)}, u32[]{:S(2)}) async-start(f32[4,2,64,512]{3,2,1,0:T(8,128)} %get-tuple-element.26), calls=%async_computation.1 | async-start | bytes 2097152 | tf_op jit(solution)/shard_map/sum_y/all_to_all | solution.py:228
  32.0 25.2 %collective-permute-start = (bf16[8,32,1920]{2,1,0:T(8,128)(2,1)}, bf16[8,32,1920]{2,1,0:T(8,128)(2,1)}, u32[]{:S(2)}, u32[]{:S(2)}) collective-permute-start(bf16[8,32,1920]{2,1,0:T(8,128)(2,1)} %get-tuple-element.25.refs_0_), channel_id=1, source_target_pairs={{0,64},{1,65},{2,66},{3,67},{8,72},{9,73},{10,74},{11,75},{16,80},... | collective-permute-start | bytes 2949128 | tf_op jit(solution)/shard_map/over_z/ppermute | solution.py:22
  50.6 9.3 %collective-permute-start.10 = (bf16[8,32,1920]{2,1,0:T(8,128)(2,1)S(1)}, bf16[8,32,1920]{2,1,0:T(8,128)(2,1)S(1)}, u32[]{:S(2)}, u32[]{:S(2)}) collective-permute-start(bf16[8,32,1920]{2,1,0:T(8,128)(2,1)S(1)} %get-tuple-element.28.right_ref.refs_2_), channel_id=1, source_target_pairs={{0,8},{1,9},{2,10},{3,11},{8,0},{9,1},{10,2},{11,3},{16,24},{17,25... | collective-permute-start | bytes 2949128 | tf_op jit(solution)/shard_map/core/ppermute | solution.py:22
  51.3 12.4 %collective-permute-start.9 = (bf16[8,32,1920]{2,1,0:T(8,128)(2,1)S(1)}, bf16[8,32,1920]{2,1,0:T(8,128)(2,1)}, u32[]{:S(2)}, u32[]{:S(2)}) collective-permute-start(bf16[8,32,1920]{2,1,0:T(8,128)(2,1)S(1)} %get-tuple-element.27.left_ref.refs_0_), channel_id=1, source_target_pairs={{0,8},{1,9},{2,10},{3,11},{8,0},{9,1},{10,2},{11,3},{16,24},{17,25... | collective-permute-start | bytes 2949128 | tf_op jit(solution)/shard_map/core/ppermute | solution.py:22
  52.9 15.2 %collective-permute-start.6 = (bf16[4,32,1920]{2,1,0:T(8,128)(2,1)}, bf16[4,32,1920]{2,1,0:T(8,128)(2,1)}, u32[]{:S(2)}, u32[]{:S(2)}) collective-permute-start(bf16[4,32,1920]{2,1,0:T(8,128)(2,1)} %get-tuple-element.29), channel_id=1, source_target_pairs={{0,16},{1,17},{2,18},{3,19},{8,24},{9,25},{10,26},{11,27},{16,32},... | collective-permute-start | bytes 1474568 | tf_op jit(solution)/shard_map/own_x2/ppermute | solution.py:22
  54.1 16.8 %collective-permute-start.7 = (bf16[4,32,1920]{2,1,0:T(8,128)(2,1)}, bf16[4,32,1920]{2,1,0:T(8,128)(2,1)}, u32[]{:S(2)}, u32[]{:S(2)}) collective-permute-start(bf16[4,32,1920]{2,1,0:T(8,128)(2,1)} %get-tuple-element.30), channel_id=1, source_target_pairs={{0,48},{1,49},{2,50},{3,51},{8,56},{9,57},{10,58},{11,59},{16,0},{... | collective-permute-start | bytes 1474568 | tf_op jit(solution)/shard_map/own_x2/ppermute | solution.py:22
  57.2 13.7 %collective-permute-start.8 = (bf16[4,32,1920]{2,1,0:T(8,128)(2,1)}, bf16[4,32,1920]{2,1,0:T(8,128)(2,1)}, u32[]{:S(2)}, u32[]{:S(2)}) collective-permute-start(bf16[4,32,1920]{2,1,0:T(8,128)(2,1)} %get-tuple-element.29), channel_id=1, source_target_pairs={{0,64},{1,65},{2,66},{3,67},{8,72},{9,73},{10,74},{11,75},{16,80},... | collective-permute-start | bytes 1474568 | tf_op jit(solution)/shard_map/dup_z/ppermute | solution.py:22
  59.9 0.9 copy-start.1
  60.8 17.8 %collective-permute-start.13 = (bf16[8,32,1920]{2,1,0:T(8,128)(2,1)}, bf16[8,32,1920]{2,1,0:T(8,128)(2,1)}, u32[]{:S(2)}, u32[]{:S(2)}) collective-permute-start(bf16[8,32,1920]{2,1,0:T(8,128)(2,1)} %collective-permute-done.refs_0_), channel_id=1, source_target_pairs={{0,8},{1,9},{2,10},{3,11},{8,0},{9,1},{10,2},{11,3},{16,24},{17,25... | collective-permute-start | bytes 2949128 | tf_op jit(solution)/shard_map/core/ppermute | solution.py:22
  63.7 14.1 %collective-permute-start.1 = (bf16[4,32,1920]{2,1,0:T(8,128)(2,1)S(1)}, bf16[4,32,1920]{2,1,0:T(8,128)(2,1)S(1)}, u32[]{:S(2)}, u32[]{:S(2)}) collective-permute-start(bf16[4,32,1920]{2,1,0:T(8,128)(2,1)S(1)} %slice.4), channel_id=1, source_target_pairs={{0,16},{1,17},{2,18},{3,19},{8,24},{9,25},{10,26},{11,27},{16,32},... | collective-permute-start | bytes 1474568 | tf_op jit(solution)/shard_map/dup_x/ppermute | solution.py:22
  63.8 1.2 %copy-start.2 = (bf16[8,32,1920]{2,1,0:T(8,128)(2,1)S(1)}, bf16[8,32,1920]{2,1,0:T(8,128)(2,1)}, u32[]{:S(2)}) copy-start(bf16[8,32,1920]{2,1,0:T(8,128)(2,1)} %copy-done.1) | copy-start | bytes 2949124
  68.2 23.9 %collective-permute-start.2 = (bf16[8,32,1920]{2,1,0:T(8,128)(2,1)}, bf16[8,32,1920]{2,1,0:T(8,128)(2,1)S(1)}, u32[]{:S(2)}, u32[]{:S(2)}) collective-permute-start(bf16[8,32,1920]{2,1,0:T(8,128)(2,1)} %collective-permute-done.refs_0_), channel_id=1, source_target_pairs={{0,48},{1,49},{2,50},{3,51},{8,56},{9,57},{10,58},{11,59},{16,0},{... | collective-permute-start | bytes 2949128 | tf_op jit(solution)/shard_map/dup_x/ppermute | solution.py:22
  70.9 7.7 %collective-permute-start.16 = (bf16[4,32,1920]{2,1,0:T(8,128)(2,1)}, bf16[4,32,1920]{2,1,0:T(8,128)(2,1)S(1)}, u32[]{:S(2)}, u32[]{:S(2)}) collective-permute-start(bf16[4,32,1920]{2,1,0:T(8,128)(2,1)} %get-tuple-element.33.refs_0_), channel_id=1, source_target_pairs={{0,8},{1,9},{2,10},{3,11},{8,0},{9,1},{10,2},{11,3},{16,24},{17,25... | collective-permute-start | bytes 1474568 | tf_op jit(solution)/shard_map/core/ppermute | solution.py:22
  72.7 15.0 %collective-permute-start.14 = (bf16[4,32,1920]{2,1,0:T(8,128)(2,1)}, bf16[4,32,1920]{2,1,0:T(8,128)(2,1)}, u32[]{:S(2)}, u32[]{:S(2)}) collective-permute-start(bf16[4,32,1920]{2,1,0:T(8,128)(2,1)} %get-tuple-element.36.refs_2_), channel_id=1, source_target_pairs={{0,8},{1,9},{2,10},{3,11},{8,0},{9,1},{10,2},{11,3},{16,24},{17,25... | collective-permute-start | bytes 1474568 | tf_op jit(solution)/shard_map/core/ppermute | solution.py:22
  77.8 9.9 %collective-permute-start.15 = (bf16[4,32,1920]{2,1,0:T(8,128)(2,1)}, bf16[4,32,1920]{2,1,0:T(8,128)(2,1)}, u32[]{:S(2)}, u32[]{:S(2)}) collective-permute-start(bf16[4,32,1920]{2,1,0:T(8,128)(2,1)} %get-tuple-element.34.refs_4_), channel_id=1, source_target_pairs={{0,8},{1,9},{2,10},{3,11},{8,0},{9,1},{10,2},{11,3},{16,24},{17,25... | collective-permute-start | bytes 1474568 | tf_op jit(solution)/shard_map/core/ppermute | solution.py:22
  78.6 14.4 %collective-permute-start.11 = (bf16[4,32,1920]{2,1,0:T(8,128)(2,1)}, bf16[4,32,1920]{2,1,0:T(8,128)(2,1)S(1)}, u32[]{:S(2)}, u32[]{:S(2)}) collective-permute-start(bf16[4,32,1920]{2,1,0:T(8,128)(2,1)} %get-tuple-element.33.refs_0_), channel_id=1, source_target_pairs={{0,16},{1,17},{2,18},{3,19},{8,24},{9,25},{10,26},{11,27},{16,32},... | collective-permute-start | bytes 1474568 | tf_op jit(solution)/shard_map/dup_x2/ppermute | solution.py:22
  78.6 0.8 copy-start.3
  79.4 15.1 %collective-permute-start.12 = (bf16[4,32,1920]{2,1,0:T(8,128)(2,1)}, bf16[4,32,1920]{2,1,0:T(8,128)(2,1)}, u32[]{:S(2)}, u32[]{:S(2)}) collective-permute-start(bf16[4,32,1920]{2,1,0:T(8,128)(2,1)} %get-tuple-element.34.refs_4_), channel_id=1, source_target_pairs={{0,64},{1,65},{2,66},{3,67},{8,72},{9,73},{10,74},{11,75},{16,80},... | collective-permute-start | bytes 1474568 | tf_op jit(solution)/shard_map/dup_z2/ppermute | solution.py:22
  84.7 1.0 copy-start.4
  94.5 5.3 %collective-permute-start.18 = (bf16[8,32,1920]{2,1,0:T(8,128)(2,1)S(1)}, bf16[8,32,1920]{2,1,0:T(8,128)(2,1)S(1)}, u32[]{:S(2)}, u32[]{:S(2)}) collective-permute-start(bf16[8,32,1920]{2,1,0:T(8,128)(2,1)S(1)} %get-tuple-element.39.refs_1_), channel_id=1, source_target_pairs={{0,8},{1,9},{2,10},{3,11},{8,0},{9,1},{10,2},{11,3},{16,24},{17,25... | collective-permute-start | bytes 2949128 | tf_op jit(solution)/shard_map/core/ppermute | solution.py:22
  95.2 3.6 %collective-permute-start.17 = (bf16[4,32,1920]{2,1,0:T(8,128)(2,1)S(1)}, bf16[4,32,1920]{2,1,0:T(8,128)(2,1)}, u32[]{:S(2)}, u32[]{:S(2)}) collective-permute-start(bf16[4,32,1920]{2,1,0:T(8,128)(2,1)S(1)} %get-tuple-element.38.refs_0_), channel_id=1, source_target_pairs={{0,8},{1,9},{2,10},{3,11},{8,0},{9,1},{10,2},{11,3},{16,24},{17,25... | collective-permute-start | bytes 1474568 | tf_op jit(solution)/shard_map/core/ppermute | solution.py:22
  95.2 4.4 %collective-permute-start.19 = (bf16[4,32,1920]{2,1,0:T(8,128)(2,1)S(1)}, bf16[4,32,1920]{2,1,0:T(8,128)(2,1)}, u32[]{:S(2)}, u32[]{:S(2)}) collective-permute-start(bf16[4,32,1920]{2,1,0:T(8,128)(2,1)S(1)} %get-tuple-element.40.refs_2_), channel_id=1, source_target_pairs={{0,8},{1,9},{2,10},{3,11},{8,0},{9,1},{10,2},{11,3},{16,24},{17,25... | collective-permute-start | bytes 1474568 | tf_op jit(solution)/shard_map/core/ppermute | solution.py:22
  95.7 4.1 %collective-permute-start.20 = (bf16[4,32,1920]{2,1,0:T(8,128)(2,1)}, bf16[4,32,1920]{2,1,0:T(8,128)(2,1)}, u32[]{:S(2)}, u32[]{:S(2)}) collective-permute-start(bf16[4,32,1920]{2,1,0:T(8,128)(2,1)} %get-tuple-element.41.refs_3_), channel_id=1, source_target_pairs={{0,8},{1,9},{2,10},{3,11},{8,0},{9,1},{10,2},{11,3},{16,24},{17,25... | collective-permute-start | bytes 1474568 | tf_op jit(solution)/shard_map/core/ppermute | solution.py:22
  95.7 6.9 %collective-permute-start.21 = (f32[64,512]{1,0:T(8,128)S(1)}, f32[64,512]{1,0:T(8,128)S(1)}, u32[]{:S(2)}, u32[]{:S(2)}) collective-permute-start(f32[64,512]{1,0:T(8,128)S(1)} %get-tuple-element.44), channel_id=1, source_target_pairs={{0,4},{1,5},{2,6},{3,7},{4,0},{5,1},{6,2},{7,3},{8,12},{9,13},{10,... | collective-permute-start | bytes 393224 | tf_op jit(solution)/shard_map/sum_z/ppermute | solution.py:259

commit v4 on v3

--- a/solution.py
+++ b/solution.py
@@ -249,8 +249,8 @@
         dup_high_2 = send(high_2, dz=2)
     total = jnp.sum(shares, axis=0)
     kept, given = pick(total, z_lo), pick(total, 1 - z_lo)
-    out = place(out, both(dup_low_1, 1 - z_hi, 1))
-    out = place(out, both(dup, 1 - z_hi, 0) + both(low_2, z_hi, 2) + both(high_2, z_hi, 2, 4))
+    out = place(out, both(dup, 1 - z_hi, 0) + both(low_2, z_hi, 2) + both(high_2, z_hi, 2, 4)
+        + both(dup_low_1, 1 - z_hi, 1))
     dup_high_1, dup_3, dup_low_2, dup_high_2, kept, given, out = fence(
         dup_high_1, dup_3, dup_low_2, dup_high_2, kept, given, out
     )

time: 104 us -> 104 us (level)
  waiting for transfers between devices: 27.5 us -> 29.1 us
  Pallas kernels: 28.7 us -> 27.2 us
    ppermute x21, waiting for transfers between devices: 14.9 us -> 16.5 us  [send(): return lax.ppermute(value, AXES, pairs)]
    pallas_call x6 -> x5, Pallas kernels: 17.3 us -> 15.8 us  [place(): pl.pallas_call(kernel, in_specs=specs, out_specs=pl.BlockSpec(memory_spac...]
  transfers between devices with their start and end apart: 24 -> 24, of which waited for: 11 -> 11; matrix products, arithmetic and copies ran while one was open for 3% -> 3% of each run, Pallas kernels for 27% -> 25%
where the time goes in v4:
time: 104 us; the launch traced here: 103 us
  starting transfers between devices  34.4 us (33%)
  waiting for transfers between devices  29.1 us (28%)
  Pallas kernels  27.2 us (26%)
  local copies, waits for them, and re-layouts  10.2 us (10%)
  other arithmetic  1.45 us (1%)
    ppermute x21, starting transfers between devices, send(): return lax.ppermute(value, AXES, pairs)  24.6 us
    ppermute x21, waiting for transfers between devices, send(): return lax.ppermute(value, AXES, pairs)  16.5 us
    pallas_call x5, Pallas kernels, place(): pl.pallas_call(kernel, in_specs=specs, out_specs=pl.BlockSpec(memory_spac...  15.8 us
    pallas_call x1, Pallas kernels, attend(): pl.pallas_call(kernel, in_specs=[pl.BlockSpec(memory_space=pltpu.SMEM), v...  8.77 us
    all_to_all x1, waiting for transfers between devices, local(): lax.all_to_all(shares, 'tp', split_axis=0, concat_axis=0, tiled=True, axi...  8.42 us
    unnamed x16, local copies, waits for them, and re-layouts  7.71 us
    all_to_all x1, starting transfers between devices, local(): own = lax.all_to_all(blocks, 'tp', split_axis=0, concat_axis=0, tiled=True)  6.37 us
    all_to_all x1, waiting for transfers between devices, local(): own = lax.all_to_all(blocks, 'tp', split_axis=0, concat_axis=0, tiled=True)  4.19 us
  transfers between devices with their start and end apart: 24, of which 11 were waited for; matrix products, arithmetic and copies ran while one was open for 3% of the time, Pallas kernels for 25%

profile of v4, /device:TPU:1, one launch (start us, length us, event | category | flops | bytes accessed | tf_op | source)
XLA Modules:
  0.0 103.3 jit_solution(5327155788397092734)
XLA Ops:
  0.6 1.5 %copy-done = f32[32,15360]{1,0:T(8,128)S(1)} copy-done((f32[32,15360]{1,0:T(8,128)S(1)}, f32[32,15360]{1,0:T(8,128)}, u32[]{:S(2)}) %copy-start) | copy-done | bytes 1966104
  2.2 1.0 %shard_map.77.after_ref = bf16[8,32,1920]{2,1,0:T(8,128)(2,1)} custom-call(f32[32,15360]{1,0:T(8,128)S(1)} %copy-done), custom_call_target="tpu_custom_call" | custom-call | tf_op jit(solution)/shard_map/pallas_call | solution.py:33
  3.2 6.4 %all-to-all-start = ((bf16[8,32,1920]{2,1,0:T(8,128)(2,1)}), bf16[8,32,1920]{2,1,0:T(8,128)(2,1)}, u32[]{:S(2)}, u32[]{:S(2)}) async-start(bf16[8,32,1920]{2,1,0:T(8,128)(2,1)} %shard_map.77.after_ref), calls=%async_computation | async-start | bytes 1966080 | tf_op jit(solution)/shard_map/over_t/all_to_all | solution.py:218
  11.8 8.8 %shard_map.78.refs_1_ = f32[4,2,64,512]{3,2,1,0:T(8,128)} custom-call(s32[8]{0:T(128)S(1)} %copy-done.7, bf16[8,8,512]{2,1,0:T(8,128)(2,1)S(1)} %copy-done.5, bf16[8,8,2,128]{3,2,1,0:T(2,128)(2,1)S(1)} %copy-done.6, bf16[8,2,1,1024,128]{4,3,2,1,0:T(8,128)(2,1)} %cache_hbm.1, bf16[512,4096]{1,0:T(8,128)(2,1)} %weight_hbm.1, ...), custom_call_target="tpu_custom_call" | custom-call | flops 1 | bytes 1 | tf_op jit(solution)/shard_map/pallas_call | solution.py:99
  20.6 4.2 %all-to-all-done.refs_0_ = bf16[8,32,1920]{2,1,0:T(8,128)(2,1)} async-done(((bf16[8,32,1920]{2,1,0:T(8,128)(2,1)}), bf16[8,32,1920]{2,1,0:T(8,128)(2,1)}, u32[]{:S(2)}, u32[]{:S(2)}) %all-to-all-start) | async-done | bytes 983072 | tf_op jit(solution)/shard_map/over_t/all_to_all | solution.py:218
  25.7 1.2 %collective-permute-start.3 = (bf16[8,32,1920]{2,1,0:T(8,128)(2,1)}, bf16[8,32,1920]{2,1,0:T(8,128)(2,1)S(1)}, u32[]{:S(2)}, u32[]{:S(2)}) collective-permute-start(bf16[8,32,1920]{2,1,0:T(8,128)(2,1)} %get-tuple-element.25.refs_0_), channel_id=1, source_target_pairs={{0,16},{1,17},{2,18},{3,19},{8,24},{9,25},{10,26},{11,27},{16,32},... | collective-permute-start | bytes 2949128 | tf_op jit(solution)/shard_map/own_x/ppermute | solution.py:22
  26.9 1.5 %collective-permute-start.4 = (bf16[8,32,1920]{2,1,0:T(8,128)(2,1)}, bf16[8,32,1920]{2,1,0:T(8,128)(2,1)S(1)}, u32[]{:S(2)}, u32[]{:S(2)}) collective-permute-start(bf16[8,32,1920]{2,1,0:T(8,128)(2,1)} %get-tuple-element.25.refs_0_), channel_id=1, source_target_pairs={{0,48},{1,49},{2,50},{3,51},{8,56},{9,57},{10,58},{11,59},{16,0},{... | collective-permute-start | bytes 2949128 | tf_op jit(solution)/shard_map/own_x/ppermute | solution.py:22
  28.3 3.5 %all-to-all-start.1 = ((f32[4,2,64,512]{3,2,1,0:T(8,128)}), f32[4,2,64,512]{3,2,1,0:T(8,128)S(1)}, u32[]{:S(2)}, u32[]{:S(2)}) async-start(f32[4,2,64,512]{3,2,1,0:T(8,128)} %get-tuple-element.26), calls=%async_computation.1 | async-start | bytes 2097152 | tf_op jit(solution)/shard_map/sum_y/all_to_all | solution.py:228
  32.0 3.3 %collective-permute-start = (bf16[8,32,1920]{2,1,0:T(8,128)(2,1)}, bf16[8,32,1920]{2,1,0:T(8,128)(2,1)}, u32[]{:S(2)}, u32[]{:S(2)}) collective-permute-start(bf16[8,32,1920]{2,1,0:T(8,128)(2,1)} %get-tuple-element.25.refs_0_), channel_id=1, source_target_pairs={{0,64},{1,65},{2,66},{3,67},{8,72},{9,73},{10,74},{11,75},{16,80},... | collective-permute-start | bytes 2949128 | tf_op jit(solution)/shard_map/over_z/ppermute | solution.py:22
  35.3 2.8 %shard_map.80.refs_3_ = bf16[2,4,2,8,32,1920]{5,4,3,2,1,0:T(8,128)(2,1)} custom-call(s32[6]{0:T(128)S(1)} %stack.35.index_ref, bf16[8,32,1920]{2,1,0:T(8,128)(2,1)} %get-tuple-element.25.refs_0_, bf16[8,32,1920]{2,1,0:T(8,128)(2,1)} %collective-permute-done.5.refs_1_), custom_call_target="tpu_custom_call" | custom-call | tf_op jit(solution)/shard_map/pallas_call | solution.py:172
  38.1 8.4 %all-to-all-done.1.refs_2_ = f32[4,2,64,512]{3,2,1,0:T(8,128)S(1)} async-done(((f32[4,2,64,512]{3,2,1,0:T(8,128)}), f32[4,2,64,512]{3,2,1,0:T(8,128)S(1)}, u32[]{:S(2)}, u32[]{:S(2)}) %all-to-all-start.1) | async-done | bytes 1048608 | tf_op jit(solution)/shard_map/sum_y/all_to_all | solution.py:228
  46.6 4.0 %collective-permute-done.3.refs_0_ = bf16[8,32,1920]{2,1,0:T(8,128)(2,1)S(1)} collective-permute-done((bf16[8,32,1920]{2,1,0:T(8,128)(2,1)}, bf16[8,32,1920]{2,1,0:T(8,128)(2,1)S(1)}, u32[]{:S(2)}, u32[]{:S(2)}) %collective-permute-start.3) | collective-permute-done | bytes 983072 | tf_op jit(solution)/shard_map/own_x/ppermute | solution.py:22
  51.3 1.6 %shard_map.82 = (bf16[4,32,1920]{2,1,0:T(8,128)(2,1)}, bf16[4,32,1920]{2,1,0:T(8,128)(2,1)}) custom-call(bf16[8,32,1920]{2,1,0:T(8,128)(2,1)S(1)} %get-tuple-element.27.left_ref.refs_0_, bf16[8,32,1920]{2,1,0:T(8,128)(2,1)S(1)} %get-tuple-element.28.right_ref.refs_2_), custom_call_target="tpu_custom_call" | custom-call | tf_op jit(solution)/shard_map/pallas_call | solution.py:140
  52.9 1.2 %collective-permute-start.6 = (bf16[4,32,1920]{2,1,0:T(8,128)(2,1)}, bf16[4,32,1920]{2,1,0:T(8,128)(2,1)}, u32[]{:S(2)}, u32[]{:S(2)}) collective-permute-start(bf16[4,32,1920]{2,1,0:T(8,128)(2,1)} %get-tuple-element.29), channel_id=1, source_target_pairs={{0,16},{1,17},{2,18},{3,19},{8,24},{9,25},{10,26},{11,27},{16,32},... | collective-permute-start | bytes 1474568 | tf_op jit(solution)/shard_map/own_x2/ppermute | solution.py:22
  54.1 1.5 %collective-permute-start.7 = (bf16[4,32,1920]{2,1,0:T(8,128)(2,1)}, bf16[4,32,1920]{2,1,0:T(8,128)(2,1)}, u32[]{:S(2)}, u32[]{:S(2)}) collective-permute-start(bf16[4,32,1920]{2,1,0:T(8,128)(2,1)} %get-tuple-element.30), channel_id=1, source_target_pairs={{0,48},{1,49},{2,50},{3,51},{8,56},{9,57},{10,58},{11,59},{16,0},{... | collective-permute-start | bytes 1474568 | tf_op jit(solution)/shard_map/own_x2/ppermute | solution.py:22
  55.7 1.6 %collective-permute-done.refs_0_ = bf16[8,32,1920]{2,1,0:T(8,128)(2,1)} collective-permute-done((bf16[8,32,1920]{2,1,0:T(8,128)(2,1)}, bf16[8,32,1920]{2,1,0:T(8,128)(2,1)}, u32[]{:S(2)}, u32[]{:S(2)}) %collective-permute-start) | collective-permute-done | bytes 983072 | tf_op jit(solution)/shard_map/over_z/ppermute | solution.py:22
  57.2 2.6 %collective-permute-start.8 = (bf16[4,32,1920]{2,1,0:T(8,128)(2,1)}, bf16[4,32,1920]{2,1,0:T(8,128)(2,1)}, u32[]{:S(2)}, u32[]{:S(2)}) collective-permute-start(bf16[4,32,1920]{2,1,0:T(8,128)(2,1)} %get-tuple-element.29), channel_id=1, source_target_pairs={{0,64},{1,65},{2,66},{3,67},{8,72},{9,73},{10,74},{11,75},{16,80},... | collective-permute-start | bytes 1474568 | tf_op jit(solution)/shard_map/dup_z/ppermute | solution.py:22
  60.8 1.7 %collective-permute-start.13 = (bf16[8,32,1920]{2,1,0:T(8,128)(2,1)}, bf16[8,32,1920]{2,1,0:T(8,128)(2,1)}, u32[]{:S(2)}, u32[]{:S(2)}) collective-permute-start(bf16[8,32,1920]{2,1,0:T(8,128)(2,1)} %collective-permute-done.refs_0_), channel_id=1, source_target_pairs={{0,8},{1,9},{2,10},{3,11},{8,0},{9,1},{10,2},{11,3},{16,24},{17,25... | collective-permute-start | bytes 2949128 | tf_op jit(solution)/shard_map/core/ppermute | solution.py:22
  62.6 1.1 %slice.4 = bf16[4,32,1920]{2,1,0:T(8,128)(2,1)S(1)} slice(bf16[8,32,1920]{2,1,0:T(8,128)(2,1)} %collective-permute-done.refs_0_), slice={[4:8], [0:32], [0:1920]} | slice | bytes 983040 | tf_op jit(solution)/shard_map/dup_x/slice | solution.py:241
  63.8 1.2 %copy-done.2 = bf16[8,32,1920]{2,1,0:T(8,128)(2,1)S(1)} copy-done((bf16[8,32,1920]{2,1,0:T(8,128)(2,1)S(1)}, bf16[8,32,1920]{2,1,0:T(8,128)(2,1)}, u32[]{:S(2)}) %copy-start.2) | copy-done | bytes 983064
  65.0 3.2 %shard_map.83.refs_4_ = bf16[2,4,2,8,32,1920]{5,4,3,2,1,0:T(8,128)(2,1)} custom-call(s32[12]{0:T(128)S(1)} %stack.36.index_ref, bf16[8,32,1920]{2,1,0:T(8,128)(2,1)S(1)} %get-tuple-element.27.left_ref.refs_0_, bf16[8,32,1920]{2,1,0:T(8,128)(2,1)} %collective-permute-done.9.refs_1_, ...), custom_call_target="tpu_custom_call", output_to_operand_aliasing={{}: (5, {})} | custom-call | tf_op jit(solution)/shard_map/pallas_call | solution.py:172
  68.2 2.7 %collective-permute-start.2 = (bf16[8,32,1920]{2,1,0:T(8,128)(2,1)}, bf16[8,32,1920]{2,1,0:T(8,128)(2,1)S(1)}, u32[]{:S(2)}, u32[]{:S(2)}) collective-permute-start(bf16[8,32,1920]{2,1,0:T(8,128)(2,1)} %collective-permute-done.refs_0_), channel_id=1, source_target_pairs={{0,48},{1,49},{2,50},{3,51},{8,56},{9,57},{10,58},{11,59},{16,0},{... | collective-permute-start | bytes 2949128 | tf_op jit(solution)/shard_map/dup_x/ppermute | solution.py:22
  70.9 1.8 %collective-permute-start.14 = (bf16[4,32,1920]{2,1,0:T(8,128)(2,1)}, bf16[4,32,1920]{2,1,0:T(8,128)(2,1)S(1)}, u32[]{:S(2)}, u32[]{:S(2)}) collective-permute-start(bf16[4,32,1920]{2,1,0:T(8,128)(2,1)} %get-tuple-element.36.refs_2_), channel_id=1, source_target_pairs={{0,8},{1,9},{2,10},{3,11},{8,0},{9,1},{10,2},{11,3},{16,24},{17,25... | collective-permute-start | bytes 1474568 | tf_op jit(solution)/shard_map/core/ppermute | solution.py:22
  72.7 5.1 %collective-permute-done.1.refs_0_ = bf16[4,32,1920]{2,1,0:T(8,128)(2,1)S(1)} collective-permute-done((bf16[4,32,1920]{2,1,0:T(8,128)(2,1)S(1)}, bf16[4,32,1920]{2,1,0:T(8,128)(2,1)S(1)}, u32[]{:S(2)}, u32[]{:S(2)}) %collective-permute-start.1) | collective-permute-done | bytes 491552 | tf_op jit(solution)/shard_map/dup_x/ppermute | solution.py:22
  79.4 3.3 %collective-permute-start.12 = (bf16[4,32,1920]{2,1,0:T(8,128)(2,1)}, bf16[4,32,1920]{2,1,0:T(8,128)(2,1)}, u32[]{:S(2)}, u32[]{:S(2)}) collective-permute-start(bf16[4,32,1920]{2,1,0:T(8,128)(2,1)} %get-tuple-element.34.refs_4_), channel_id=1, source_target_pairs={{0,64},{1,65},{2,66},{3,67},{8,72},{9,73},{10,74},{11,75},{16,80},... | collective-permute-start | bytes 1474568 | tf_op jit(solution)/shard_map/dup_z2/ppermute | solution.py:22
  83.6 1.0 dynamic-slice_bitcast_fusion
  84.6 1.0 copy-done.4
  85.6 4.5 %shard_map.85.refs_6_ = bf16[2,4,2,8,32,1920]{5,4,3,2,1,0:T(8,128)(2,1)} custom-call(s32[24]{0:T(128)S(1)} %stack.37.index_ref, bf16[8,32,1920]{2,1,0:T(8,128)(2,1)} %collective-permute-done.refs_0_, bf16[8,32,1920]{2,1,0:T(8,128)(2,1)} %collective-permute-done.13.refs_1_, ...), custom_call_target="tpu_custom_call", output_to_operand_aliasing={{}: (9, {})} | custom-call | tf_op jit(solution)/shard_map/pallas_call | solution.py:172
  90.2 1.9 %collective-permute-done.2.refs_1_ = bf16[8,32,1920]{2,1,0:T(8,128)(2,1)S(1)} collective-permute-done((bf16[8,32,1920]{2,1,0:T(8,128)(2,1)}, bf16[8,32,1920]{2,1,0:T(8,128)(2,1)S(1)}, u32[]{:S(2)}, u32[]{:S(2)}) %collective-permute-start.2) | collective-permute-done | bytes 983072 | tf_op jit(solution)/shard_map/dup_x/ppermute | solution.py:22
  93.0 1.5 %collective-permute-done.12.refs_3_ = bf16[4,32,1920]{2,1,0:T(8,128)(2,1)} collective-permute-done((bf16[4,32,1920]{2,1,0:T(8,128)(2,1)}, bf16[4,32,1920]{2,1,0:T(8,128)(2,1)}, u32[]{:S(2)}, u32[]{:S(2)}) %collective-permute-start.12) | collective-permute-done | bytes 491552 | tf_op jit(solution)/shard_map/dup_z2/ppermute | solution.py:22
  95.9 2.5 %shard_map.87.refs_4_ = bf16[2,4,2,8,32,1920]{5,4,3,2,1,0:T(8,128)(2,1)} custom-call(s32[12]{0:T(128)S(1)} %stack.38.index_ref, bf16[4,32,1920]{2,1,0:T(8,128)(2,1)S(1)} %get-tuple-element.38.refs_0_, bf16[8,32,1920]{2,1,0:T(8,128)(2,1)S(1)} %get-tuple-element.39.refs_1_, ...), custom_call_target="tpu_custom_call", output_to_operand_aliasing={{}: (5, {})} | custom-call | tf_op jit(solution)/shard_map/pallas_call | solution.py:172
  99.8 2.8 %shard_map.88.refs_0_ = bf16[2,4,2,8,32,1920]{5,4,3,2,1,0:T(8,128)(2,1)} custom-call(s32[12]{0:T(128)S(1)} %stack.31.index_ref, bf16[4,32,1920]{2,1,0:T(8,128)(2,1)} %collective-permute-done.17.refs_0_, bf16[8,32,1920]{2,1,0:T(8,128)(2,1)S(1)} %collective-permute-done.18.refs_1_, ...), custom_call_target="tpu_custom_call", output_to_operand_aliasing={{}: (5, {})} | custom-call | tf_op jit(solution)/shard_map/pallas_call | solution.py:172
  (55 shorter events, 11.9 us)
Async XLA Ops:
  0.6 1.5 %copy-start = (f32[32,15360]{1,0:T(8,128)S(1)}, f32[32,15360]{1,0:T(8,128)}, u32[]{:S(2)}) copy-start(f32[32,15360]{1,0:T(8,128)} %in_ref.1) | copy-start | bytes 5898244
  3.2 21.6 %all-to-all-start = ((bf16[8,32,1920]{2,1,0:T(8,128)(2,1)}), bf16[8,32,1920]{2,1,0:T(8,128)(2,1)}, u32[]{:S(2)}, u32[]{:S(2)}) async-start(bf16[8,32,1920]{2,1,0:T(8,128)(2,1)} %shard_map.77.after_ref), calls=%async_computation | async-start | bytes 1966080 | tf_op jit(solution)/shard_map/over_t/all_to_all | solution.py:218
  9.6 0.8 copy-start.5
  10.4 0.8 copy-start.6
  11.2 0.7 copy-start.7
  24.8 10.5 %collective-permute-start.5 = (bf16[8,32,1920]{2,1,0:T(8,128)(2,1)}, bf16[8,32,1920]{2,1,0:T(8,128)(2,1)}, u32[]{:S(2)}, u32[]{:S(2)}) collective-permute-start(bf16[8,32,1920]{2,1,0:T(8,128)(2,1)} %get-tuple-element.25.refs_0_), channel_id=1, source_target_pairs={{0,8},{1,9},{2,10},{3,11},{8,0},{9,1},{10,2},{11,3},{16,24},{17,25... | collective-permute-start | bytes 2949128 | tf_op jit(solution)/shard_map/core/ppermute | solution.py:22
  25.7 24.9 %collective-permute-start.3 = (bf16[8,32,1920]{2,1,0:T(8,128)(2,1)}, bf16[8,32,1920]{2,1,0:T(8,128)(2,1)S(1)}, u32[]{:S(2)}, u32[]{:S(2)}) collective-permute-start(bf16[8,32,1920]{2,1,0:T(8,128)(2,1)} %get-tuple-element.25.refs_0_), channel_id=1, source_target_pairs={{0,16},{1,17},{2,18},{3,19},{8,24},{9,25},{10,26},{11,27},{16,32},... | collective-permute-start | bytes 2949128 | tf_op jit(solution)/shard_map/own_x/ppermute | solution.py:22
  26.9 23.7 %collective-permute-start.4 = (bf16[8,32,1920]{2,1,0:T(8,128)(2,1)}, bf16[8,32,1920]{2,1,0:T(8,128)(2,1)S(1)}, u32[]{:S(2)}, u32[]{:S(2)}) collective-permute-start(bf16[8,32,1920]{2,1,0:T(8,128)(2,1)} %get-tuple-element.25.refs_0_), channel_id=1, source_target_pairs={{0,48},{1,49},{2,50},{3,51},{8,56},{9,57},{10,58},{11,59},{16,0},{... | collective-permute-start | bytes 2949128 | tf_op jit(solution)/shard_map/own_x/ppermute | solution.py:22
  28.3 18.2 %all-to-all-start.1 = ((f32[4,2,64,512]{3,2,1,0:T(8,128)}), f32[4,2,64,512]{3,2,1,0:T(8,128)S(1)}, u32[]{:S(2)}, u32[]{:S(2)}) async-start(f32[4,2,64,512]{3,2,1,0:T(8,128)} %get-tuple-element.26), calls=%async_computation.1 | async-start | bytes 2097152 | tf_op jit(solution)/shard_map/sum_y/all_to_all | solution.py:228
  32.0 25.2 %collective-permute-start = (bf16[8,32,1920]{2,1,0:T(8,128)(2,1)}, bf16[8,32,1920]{2,1,0:T(8,128)(2,1)}, u32[]{:S(2)}, u32[]{:S(2)}) collective-permute-start(bf16[8,32,1920]{2,1,0:T(8,128)(2,1)} %get-tuple-element.25.refs_0_), channel_id=1, source_target_pairs={{0,64},{1,65},{2,66},{3,67},{8,72},{9,73},{10,74},{11,75},{16,80},... | collective-permute-start | bytes 2949128 | tf_op jit(solution)/shard_map/over_z/ppermute | solution.py:22
  50.6 9.3 %collective-permute-start.10 = (bf16[8,32,1920]{2,1,0:T(8,128)(2,1)S(1)}, bf16[8,32,1920]{2,1,0:T(8,128)(2,1)S(1)}, u32[]{:S(2)}, u32[]{:S(2)}) collective-permute-start(bf16[8,32,1920]{2,1,0:T(8,128)(2,1)S(1)} %get-tuple-element.28.right_ref.refs_2_), channel_id=1, source_target_pairs={{0,8},{1,9},{2,10},{3,11},{8,0},{9,1},{10,2},{11,3},{16,24},{17,25... | collective-permute-start | bytes 2949128 | tf_op jit(solution)/shard_map/core/ppermute | solution.py:22
  51.3 12.4 %collective-permute-start.9 = (bf16[8,32,1920]{2,1,0:T(8,128)(2,1)S(1)}, bf16[8,32,1920]{2,1,0:T(8,128)(2,1)}, u32[]{:S(2)}, u32[]{:S(2)}) collective-permute-start(bf16[8,32,1920]{2,1,0:T(8,128)(2,1)S(1)} %get-tuple-element.27.left_ref.refs_0_), channel_id=1, source_target_pairs={{0,8},{1,9},{2,10},{3,11},{8,0},{9,1},{10,2},{11,3},{16,24},{17,25... | collective-permute-start | bytes 2949128 | tf_op jit(solution)/shard_map/core/ppermute | solution.py:22
  52.9 15.2 %collective-permute-start.6 = (bf16[4,32,1920]{2,1,0:T(8,128)(2,1)}, bf16[4,32,1920]{2,1,0:T(8,128)(2,1)}, u32[]{:S(2)}, u32[]{:S(2)}) collective-permute-start(bf16[4,32,1920]{2,1,0:T(8,128)(2,1)} %get-tuple-element.29), channel_id=1, source_target_pairs={{0,16},{1,17},{2,18},{3,19},{8,24},{9,25},{10,26},{11,27},{16,32},... | collective-permute-start | bytes 1474568 | tf_op jit(solution)/shard_map/own_x2/ppermute | solution.py:22
  54.1 16.8 %collective-permute-start.7 = (bf16[4,32,1920]{2,1,0:T(8,128)(2,1)}, bf16[4,32,1920]{2,1,0:T(8,128)(2,1)}, u32[]{:S(2)}, u32[]{:S(2)}) collective-permute-start(bf16[4,32,1920]{2,1,0:T(8,128)(2,1)} %get-tuple-element.30), channel_id=1, source_target_pairs={{0,48},{1,49},{2,50},{3,51},{8,56},{9,57},{10,58},{11,59},{16,0},{... | collective-permute-start | bytes 1474568 | tf_op jit(solution)/shard_map/own_x2/ppermute | solution.py:22
  57.2 13.7 %collective-permute-start.8 = (bf16[4,32,1920]{2,1,0:T(8,128)(2,1)}, bf16[4,32,1920]{2,1,0:T(8,128)(2,1)}, u32[]{:S(2)}, u32[]{:S(2)}) collective-permute-start(bf16[4,32,1920]{2,1,0:T(8,128)(2,1)} %get-tuple-element.29), channel_id=1, source_target_pairs={{0,64},{1,65},{2,66},{3,67},{8,72},{9,73},{10,74},{11,75},{16,80},... | collective-permute-start | bytes 1474568 | tf_op jit(solution)/shard_map/dup_z/ppermute | solution.py:22
  59.9 0.9 copy-start.1
  60.8 17.8 %collective-permute-start.13 = (bf16[8,32,1920]{2,1,0:T(8,128)(2,1)}, bf16[8,32,1920]{2,1,0:T(8,128)(2,1)}, u32[]{:S(2)}, u32[]{:S(2)}) collective-permute-start(bf16[8,32,1920]{2,1,0:T(8,128)(2,1)} %collective-permute-done.refs_0_), channel_id=1, source_target_pairs={{0,8},{1,9},{2,10},{3,11},{8,0},{9,1},{10,2},{11,3},{16,24},{17,25... | collective-permute-start | bytes 2949128 | tf_op jit(solution)/shard_map/core/ppermute | solution.py:22
  63.7 14.1 %collective-permute-start.1 = (bf16[4,32,1920]{2,1,0:T(8,128)(2,1)S(1)}, bf16[4,32,1920]{2,1,0:T(8,128)(2,1)S(1)}, u32[]{:S(2)}, u32[]{:S(2)}) collective-permute-start(bf16[4,32,1920]{2,1,0:T(8,128)(2,1)S(1)} %slice.4), channel_id=1, source_target_pairs={{0,16},{1,17},{2,18},{3,19},{8,24},{9,25},{10,26},{11,27},{16,32},... | collective-permute-start | bytes 1474568 | tf_op jit(solution)/shard_map/dup_x/ppermute | solution.py:22
  63.8 1.2 %copy-start.2 = (bf16[8,32,1920]{2,1,0:T(8,128)(2,1)S(1)}, bf16[8,32,1920]{2,1,0:T(8,128)(2,1)}, u32[]{:S(2)}) copy-start(bf16[8,32,1920]{2,1,0:T(8,128)(2,1)} %copy-done.1) | copy-start | bytes 2949124
  68.2 23.9 %collective-permute-start.2 = (bf16[8,32,1920]{2,1,0:T(8,128)(2,1)}, bf16[8,32,1920]{2,1,0:T(8,128)(2,1)S(1)}, u32[]{:S(2)}, u32[]{:S(2)}) collective-permute-start(bf16[8,32,1920]{2,1,0:T(8,128)(2,1)} %collective-permute-done.refs_0_), channel_id=1, source_target_pairs={{0,48},{1,49},{2,50},{3,51},{8,56},{9,57},{10,58},{11,59},{16,0},{... | collective-permute-start | bytes 2949128 | tf_op jit(solution)/shard_map/dup_x/ppermute | solution.py:22
  70.9 7.7 %collective-permute-start.14 = (bf16[4,32,1920]{2,1,0:T(8,128)(2,1)}, bf16[4,32,1920]{2,1,0:T(8,128)(2,1)S(1)}, u32[]{:S(2)}, u32[]{:S(2)}) collective-permute-start(bf16[4,32,1920]{2,1,0:T(8,128)(2,1)} %get-tuple-element.36.refs_2_), channel_id=1, source_target_pairs={{0,8},{1,9},{2,10},{3,11},{8,0},{9,1},{10,2},{11,3},{16,24},{17,25... | collective-permute-start | bytes 1474568 | tf_op jit(solution)/shard_map/core/ppermute | solution.py:22
  72.7 11.9 %collective-permute-start.15 = (bf16[4,32,1920]{2,1,0:T(8,128)(2,1)}, bf16[4,32,1920]{2,1,0:T(8,128)(2,1)}, u32[]{:S(2)}, u32[]{:S(2)}) collective-permute-start(bf16[4,32,1920]{2,1,0:T(8,128)(2,1)} %get-tuple-element.34.refs_4_), channel_id=1, source_target_pairs={{0,8},{1,9},{2,10},{3,11},{8,0},{9,1},{10,2},{11,3},{16,24},{17,25... | collective-permute-start | bytes 1474568 | tf_op jit(solution)/shard_map/core/ppermute | solution.py:22
  77.8 6.8 %collective-permute-start.16 = (bf16[4,32,1920]{2,1,0:T(8,128)(2,1)}, bf16[4,32,1920]{2,1,0:T(8,128)(2,1)}, u32[]{:S(2)}, u32[]{:S(2)}) collective-permute-start(bf16[4,32,1920]{2,1,0:T(8,128)(2,1)} %get-tuple-element.33.refs_6_), channel_id=1, source_target_pairs={{0,8},{1,9},{2,10},{3,11},{8,0},{9,1},{10,2},{11,3},{16,24},{17,25... | collective-permute-start | bytes 1474568 | tf_op jit(solution)/shard_map/core/ppermute | solution.py:22
  78.6 14.4 %collective-permute-start.11 = (bf16[4,32,1920]{2,1,0:T(8,128)(2,1)}, bf16[4,32,1920]{2,1,0:T(8,128)(2,1)S(1)}, u32[]{:S(2)}, u32[]{:S(2)}) collective-permute-start(bf16[4,32,1920]{2,1,0:T(8,128)(2,1)} %get-tuple-element.33.refs_6_), channel_id=1, source_target_pairs={{0,16},{1,17},{2,18},{3,19},{8,24},{9,25},{10,26},{11,27},{16,32},... | collective-permute-start | bytes 1474568 | tf_op jit(solution)/shard_map/dup_x2/ppermute | solution.py:22
  78.6 0.8 copy-start.3
  79.4 15.1 %collective-permute-start.12 = (bf16[4,32,1920]{2,1,0:T(8,128)(2,1)}, bf16[4,32,1920]{2,1,0:T(8,128)(2,1)}, u32[]{:S(2)}, u32[]{:S(2)}) collective-permute-start(bf16[4,32,1920]{2,1,0:T(8,128)(2,1)} %get-tuple-element.34.refs_4_), channel_id=1, source_target_pairs={{0,64},{1,65},{2,66},{3,67},{8,72},{9,73},{10,74},{11,75},{16,80},... | collective-permute-start | bytes 1474568 | tf_op jit(solution)/shard_map/dup_z2/ppermute | solution.py:22
  84.6 1.0 copy-start.4
  94.5 5.3 %collective-permute-start.18 = (bf16[8,32,1920]{2,1,0:T(8,128)(2,1)S(1)}, bf16[8,32,1920]{2,1,0:T(8,128)(2,1)S(1)}, u32[]{:S(2)}, u32[]{:S(2)}) collective-permute-start(bf16[8,32,1920]{2,1,0:T(8,128)(2,1)S(1)} %get-tuple-element.39.refs_1_), channel_id=1, source_target_pairs={{0,8},{1,9},{2,10},{3,11},{8,0},{9,1},{10,2},{11,3},{16,24},{17,25... | collective-permute-start | bytes 2949128 | tf_op jit(solution)/shard_map/core/ppermute | solution.py:22
  95.2 3.6 %collective-permute-start.17 = (bf16[4,32,1920]{2,1,0:T(8,128)(2,1)S(1)}, bf16[4,32,1920]{2,1,0:T(8,128)(2,1)}, u32[]{:S(2)}, u32[]{:S(2)}) collective-permute-start(bf16[4,32,1920]{2,1,0:T(8,128)(2,1)S(1)} %get-tuple-element.38.refs_0_), channel_id=1, source_target_pairs={{0,8},{1,9},{2,10},{3,11},{8,0},{9,1},{10,2},{11,3},{16,24},{17,25... | collective-permute-start | bytes 1474568 | tf_op jit(solution)/shard_map/core/ppermute | solution.py:22
  95.2 4.4 %collective-permute-start.19 = (bf16[4,32,1920]{2,1,0:T(8,128)(2,1)S(1)}, bf16[4,32,1920]{2,1,0:T(8,128)(2,1)}, u32[]{:S(2)}, u32[]{:S(2)}) collective-permute-start(bf16[4,32,1920]{2,1,0:T(8,128)(2,1)S(1)} %get-tuple-element.40.refs_2_), channel_id=1, source_target_pairs={{0,8},{1,9},{2,10},{3,11},{8,0},{9,1},{10,2},{11,3},{16,24},{17,25... | collective-permute-start | bytes 1474568 | tf_op jit(solution)/shard_map/core/ppermute | solution.py:22
  95.7 4.1 %collective-permute-start.20 = (bf16[4,32,1920]{2,1,0:T(8,128)(2,1)}, bf16[4,32,1920]{2,1,0:T(8,128)(2,1)}, u32[]{:S(2)}, u32[]{:S(2)}) collective-permute-start(bf16[4,32,1920]{2,1,0:T(8,128)(2,1)} %get-tuple-element.41.refs_3_), channel_id=1, source_target_pairs={{0,8},{1,9},{2,10},{3,11},{8,0},{9,1},{10,2},{11,3},{16,24},{17,25... | collective-permute-start | bytes 1474568 | tf_op jit(solution)/shard_map/core/ppermute | solution.py:22
  95.7 6.9 %collective-permute-start.21 = (f32[64,512]{1,0:T(8,128)S(1)}, f32[64,512]{1,0:T(8,128)S(1)}, u32[]{:S(2)}, u32[]{:S(2)}) collective-permute-start(f32[64,512]{1,0:T(8,128)S(1)} %get-tuple-element.44), channel_id=1, source_target_pairs={{0,4},{1,5},{2,6},{3,7},{4,0},{5,1},{6,2},{7,3},{8,12},{9,13},{10,... | collective-permute-start | bytes 393224 | tf_op jit(solution)/shard_map/sum_z/ppermute | solution.py:259
